TPU v7x, 128 devices: a whole 4x4x4 slice. The times are simulated.
128 devices in a mesh: section: 2 (over core), ep: 64 (over y, x, z).
Axes of the slice: x: 4, y: 4, z: 4, core: 2. Of those that a mesh axis runs over, the one named last changes fastest.
Arguments:
- top_grads: bfloat16 [2, 4096, 1536], P(None, 'ep'), may hold values from -6 to 6
- expert_ids: int32 [2, 2, 4096, 4], P('section', None, 'ep'), may hold values from 0 to 63, as said below
- route_weights: float32 [2, 2, 4096, 4], P('section', None, 'ep'), may hold values from 0.05 to 0.6
- preacts: bfloat16 [2, 2, 64, 384, 3072], P('section', None, 'ep'), may hold values from -6 to 6
- w_gate_up: bfloat16 [2, 64, 1536, 3072], P('section', 'ep'), may hold values from -0.15625 to 0.15625
- w_down: bfloat16 [2, 64, 1536, 1536], P('section', 'ep'), may hold values from -0.15625 to 0.15625
Outputs:
- input_grads: bfloat16 [2, 2, 4096, 1536], P('section', None, 'ep')
Inputs may be any that keep to these rules, and one draw needn't show every extreme that they name: `expert_ids`: each row names 4 different experts. Among the rows of one block of 64 tokens of one layer and micro-batch no expert is named more than 6 times, and in each layer and micro-batch some expert is named exactly 6 times in every block.
All inputs are finite; a program needn't handle non-finite values.
Results may differ from a plain program's by a relative error of at most 0.007.
Values may be sent and summed in bfloat16 or wider, within the bound.
No kernel may reach another device: no remote copies, remote signals or barrier semaphores. Data moves between devices by JAX's collectives and lax.ppermute only.
A program may use at most 128 MiB of HBM per device.

v0:
```python
import jax
import jax.numpy as jnp
from jax import lax
from jax.sharding import PartitionSpec as P

alpha_glu = 1.702


def passed_along(value, axis, steps):
    count = lax.axis_size(axis)
    initial, last = (max(0, -steps), min(count, count - steps))
    return lax.ppermute(value, axis, [(source, source + steps) for source in range(initial, last)])


def expert_rows(saved, grad_rows, w_gate_up, w_down):
    hidden = w_down.shape[0]
    back_grad = lax.dot_general(
        grad_rows, w_down, (((1,), (1,)), ((), ())), preferred_element_type=jnp.float32
    )
    gate_pre = saved[:, :hidden].astype(jnp.float32)
    up_pre = saved[:, hidden:].astype(jnp.float32)
    sigmoid_gate = jax.nn.sigmoid(alpha_glu * gate_pre)
    up_grad = (back_grad * gate_pre * sigmoid_gate).astype(jnp.bfloat16)
    gate_grad = (
        back_grad
        * (up_pre + 1.0)
        * sigmoid_gate
        * (1.0 + alpha_glu * gate_pre * (1.0 - sigmoid_gate))
    ).astype(jnp.bfloat16)
    joined = jnp.concatenate([gate_grad, up_grad], axis=1)
    return lax.dot_general(
        joined, w_gate_up, (((1,), (1,)), ((), ())), preferred_element_type=jnp.float32
    ).astype(jnp.bfloat16)


def layer_grads(incoming, chosen_ids, pick_weights, saved, w_gate_up, w_down):
    device_count = lax.axis_size("ep")
    micro_count, token_count, top_count = chosen_ids.shape
    model_width = incoming.shape[2]
    capacity = 3 * token_count * top_count // (2 * device_count)
    slot_count = device_count * capacity
    pick_count = token_count * top_count
    flat_ids = chosen_ids.reshape(micro_count, pick_count)
    expert_hot = (flat_ids[..., None] == jnp.arange(device_count, dtype=jnp.int32)).astype(
        jnp.bfloat16
    )
    positions = jnp.arange(pick_count, dtype=jnp.int32)
    strictly_before = (positions[:, None] > positions[None, :]).astype(jnp.bfloat16)
    earlier = jnp.einsum(
        "pq,mqe->mpe", strictly_before, expert_hot, preferred_element_type=jnp.float32
    )
    slot_index = jnp.sum(earlier * expert_hot.astype(jnp.float32), axis=-1).astype(jnp.int32)
    targets = flat_ids * capacity + slot_index
    slot_range = jnp.arange(slot_count, dtype=jnp.int32)
    slot_hot = (targets[..., None] == slot_range).astype(jnp.bfloat16)
    scaled = (
        (pick_weights[..., None] * incoming[:, :, None, :].astype(jnp.float32))
        .astype(jnp.bfloat16)
        .reshape(micro_count, pick_count, model_width)
    )
    outgoing = jnp.einsum(
        "mps,mpd->msd", slot_hot, scaled, preferred_element_type=jnp.float32
    ).astype(jnp.bfloat16)
    arrived = lax.all_to_all(
        outgoing.reshape(micro_count, device_count, capacity, model_width),
        "ep",
        split_axis=1,
        concat_axis=1,
        tiled=True,
    )
    answers = expert_rows(
        saved.reshape(micro_count * slot_count, saved.shape[-1]),
        arrived.reshape(micro_count * slot_count, model_width),
        w_gate_up,
        w_down,
    )
    returned = lax.all_to_all(
        answers.reshape(micro_count, device_count, capacity, model_width),
        "ep",
        split_axis=1,
        concat_axis=1,
        tiled=True,
    )
    token_targets = targets.reshape(micro_count, token_count, top_count)
    token_hot = jnp.any(token_targets[..., None] == slot_range, axis=2).astype(jnp.bfloat16)
    gathered = jnp.einsum(
        "mts,msd->mtd",
        token_hot,
        returned.reshape(micro_count, slot_count, model_width),
        preferred_element_type=jnp.float32,
    )
    summed = incoming.astype(jnp.float32) + gathered
    return summed.astype(jnp.bfloat16)


def body(top_grads, expert_ids, route_weights, preacts, w_gate_up, w_down):
    section_count = lax.axis_size("section")
    section_index = lax.axis_index("section")
    chosen_ids = expert_ids[0]
    pick_weights = route_weights[0]
    saved = preacts[0, :, 0]
    weight_in = w_gate_up[0, 0]
    weight_out = w_down[0, 0]
    own_grads = jnp.zeros_like(top_grads)
    incoming = top_grads
    for step_index in range(section_count):
        layer_out = layer_grads(incoming, chosen_ids, pick_weights, saved, weight_in, weight_out)
        own_grads = jnp.where(section_index == section_count - 1 - step_index, layer_out, own_grads)
        if step_index + 1 < section_count:
            incoming = passed_along(layer_out, "section", -1)
    return own_grads[None]


def solution(mesh):
    placed = (
        P(None, "ep", None),
        P("section", None, "ep", None),
        P("section", None, "ep", None),
        P("section", None, "ep", None, None),
        P("section", "ep", None, None),
        P("section", "ep", None, None),
    )
    return jax.shard_map(
        body, mesh=mesh, in_specs=placed, out_specs=P("section", None, "ep", None), check_vma=False
    )
```

profile of v0, /device:TPU:1, one launch (start us, length us, event | category | flops | bytes accessed | tf_op | source)
XLA Modules:
  0.0 243.4 jit_solution(495289187739384261)
XLA Ops:
  0.0 0.8 copy.30
  0.8 0.0 copy-start.1
  0.8 0.1 eq.25
  0.9 0.2 fusion.45
  1.2 0.8 copy.33
  1.9 0.1 mul.97
  2.1 0.0 copy-done.1
  2.1 3.0 %mul.99 = f32[2,64,4,1536]{3,2,1,0:T(4,128)} broadcast(bf16[2,64,1536]{2,1,0:T(8,128)(2,1)} %param.6), dimensions={0,1,3} | broadcast | bytes 3538944 | tf_op jit(solution)/shard_map/mul | solution.py:57
  5.1 3.2 %mul.100 = f32[2,256,1536]{2,1,0:T(8,128)S(1)} reshape(f32[2,64,4,1536]{3,2,1,0:T(4,128)} %mul.99) | data formatting | bytes 6291456 | tf_op jit(solution)/shard_map/mul | solution.py:57
  8.3 0.9 convolution_convert_fusion.1
  9.2 2.4 copy.34
  11.6 43.5 %all_to_all.20 = bf16[2,64,6,1536]{3,0,2,1:T(2,128)(2,1)S(1)} all-to-all(bf16[2,64,6,1536]{3,0,2,1:T(2,128)(2,1)S(1)} %bitcast.45), channel_id=1, replica_groups=mesh['section'=2,'ep'=64] {'ep'}, dimensions={1} | all-to-all | bytes 4718592 | tf_op jit(solution)/shard_map/all_to_all | solution.py:64
  55.1 0.5 copy.35
  55.6 2.3 reshape.62
  57.9 10.1 %multiply_convert_fusion.1 = (bf16[768,1536]{1,0:T(8,128)(2,1)S(1)}, bf16[768,1536]{1,0:T(8,128)(2,1)S(1)}) fusion(bf16[768,3072]{1,0:T(8,128)(2,1)} %bitcast.48, bf16[768,1536]{1,0:T(8,128)(2,1)} %reshape.62, bf16[1,1,1536,1536]{3,2,1,0:T(8,128)(2,1)} %param.11), kind=kOutput, calls=%fused_computation.28 | convolution fusion | flops 3643932672 | bytes 16515072 | tf_op jit(solution)/shard_map/dot_general | solution.py:17
  68.0 11.1 %fusion.24 = bf16[768,1536]{1,0:T(8,128)(2,1)} fusion(bf16[1,1,1536,3072]{3,2,1,0:T(8,128)(2,1)} %param.10, bf16[768,1536]{1,0:T(8,128)(2,1)S(1)} %get-tuple-element.8, bf16[768,1536]{1,0:T(8,128)(2,1)S(1)} %get-tuple-element.7), kind=kOutput, calls=%fused_computation.32 | convolution fusion | flops 7258374144 | bytes 16515072 | tf_op jit(solution)/shard_map/dot_general | solution.py:31
  79.1 3.5 %reshape.63 = bf16[2,64,6,1536]{3,2,1,0:T(8,128)(2,1)S(1)} reshape(bf16[768,1536]{1,0:T(8,128)(2,1)} %fusion.24) | data formatting | bytes 4718592 | tf_op jit(solution)/shard_map/reshape | solution.py:78
  82.7 0.0 copy-start
  82.7 3.8 %copy.36 = bf16[2,64,6,1536]{3,0,2,1:T(2,128)(2,1)} copy(bf16[2,64,6,1536]{3,2,1,0:T(8,128)(2,1)S(1)} %reshape.63) | data formatting | bytes 4718592 | tf_op jit(solution)/shard_map/reshape | solution.py:78
  86.5 0.0 copy-start.2
  86.5 5.5 %all-to-all-start.1 = ((bf16[2,64,6,1536]{3,0,2,1:T(2,128)(2,1)}), bf16[2,64,6,1536]{3,0,2,1:T(2,128)(2,1)S(1)}, u32[]{:S(2)}, u32[]{:S(2)}) async-start(bf16[2,64,6,1536]{3,0,2,1:T(2,128)(2,1)} %copy.36), calls=%async_computation.1 | async-start | bytes 4718592 | tf_op jit(solution)/shard_map/all_to_all | solution.py:77
  92.1 0.1 convert_element_type.89
  92.2 0.0 copy-done.2
  92.2 0.1 copy.32
  92.3 0.2 fusion.46
  92.5 0.0 copy-start.7
  92.5 29.2 %all-to-all-done.1 = bf16[2,64,6,1536]{3,0,2,1:T(2,128)(2,1)S(1)} async-done(((bf16[2,64,6,1536]{3,0,2,1:T(2,128)(2,1)}), bf16[2,64,6,1536]{3,0,2,1:T(2,128)(2,1)S(1)}, u32[]{:S(2)}, u32[]{:S(2)}) %all-to-all-start.1) | async-done | bytes 2359328 | tf_op jit(solution)/shard_map/all_to_all | solution.py:77
  121.6 0.0 copy-done
  121.6 0.5 fusion.34
  122.2 0.0 copy-start.3
  122.2 5.9 %collective-permute-start = (bf16[2,64,1536]{2,1,0:T(8,128)(2,1)S(1)}, bf16[2,64,1536]{2,1,0:T(8,128)(2,1)S(1)}, u32[]{:S(2)}, u32[]{:S(2)}) collective-permute-start(bf16[2,64,1536]{2,1,0:T(8,128)(2,1)S(1)} %fusion.34), channel_id=1, source_target_pairs={{64,0},{65,1},{66,2},{67,3},{68,4},{69,5},{70,6},{71,7},{72,8},{73... | collective-permute-start | bytes 1179656 | tf_op jit(solution)/shard_map/ppermute | solution.py:12
  128.1 1.1 collective-permute-done
  129.2 0.0 copy-done.7
  129.2 0.0 copy-done.3
  129.2 0.0 copy-start.5
  129.2 0.8 copy-done.5
  129.9 2.0 mul.109
  132.0 3.2 %mul.110 = f32[2,256,1536]{2,1,0:T(8,128)S(1)} reshape(f32[2,64,4,1536]{3,2,1,0:T(4,128)} %mul.109) | data formatting | bytes 6291456 | tf_op jit(solution)/shard_map/mul | solution.py:57
  135.2 0.9 convolution_convert_fusion
  136.0 2.4 copy.38
  138.5 37.1 %all_to_all.21 = bf16[2,64,6,1536]{3,0,2,1:T(2,128)(2,1)S(1)} all-to-all(bf16[2,64,6,1536]{3,0,2,1:T(2,128)(2,1)S(1)} %bitcast.46), channel_id=1, replica_groups=mesh['section'=2,'ep'=64] {'ep'}, dimensions={1} | all-to-all | bytes 4718592 | tf_op jit(solution)/shard_map/all_to_all | solution.py:64
  175.6 0.5 copy.39
  176.1 2.3 reshape.66
  178.3 10.1 %multiply_convert_fusion = (bf16[768,1536]{1,0:T(8,128)(2,1)S(1)}, bf16[768,1536]{1,0:T(8,128)(2,1)S(1)}) fusion(bf16[768,3072]{1,0:T(8,128)(2,1)} %bitcast.49, bf16[768,1536]{1,0:T(8,128)(2,1)} %reshape.66, bf16[1,1,1536,1536]{3,2,1,0:T(8,128)(2,1)} %param.11), kind=kOutput, calls=%fused_computation.27 | convolution fusion | flops 3643932672 | bytes 16515072 | tf_op jit(solution)/shard_map/dot_general | solution.py:17
  188.4 11.1 %fusion.29 = bf16[768,1536]{1,0:T(8,128)(2,1)} fusion(bf16[1,1,1536,3072]{3,2,1,0:T(8,128)(2,1)} %param.10, bf16[768,1536]{1,0:T(8,128)(2,1)S(1)} %get-tuple-element.6, bf16[768,1536]{1,0:T(8,128)(2,1)S(1)} %get-tuple-element.5), kind=kOutput, calls=%fused_computation.33 | convolution fusion | flops 7258374144 | bytes 16515072 | tf_op jit(solution)/shard_map/dot_general | solution.py:31
  199.5 3.5 %reshape.67 = bf16[2,64,6,1536]{3,2,1,0:T(8,128)(2,1)S(1)} reshape(bf16[768,1536]{1,0:T(8,128)(2,1)} %fusion.29) | data formatting | bytes 4718592 | tf_op jit(solution)/shard_map/reshape | solution.py:78
  203.1 0.0 copy-start.4
  203.1 3.8 %copy.40 = bf16[2,64,6,1536]{3,0,2,1:T(2,128)(2,1)} copy(bf16[2,64,6,1536]{3,2,1,0:T(8,128)(2,1)S(1)} %reshape.67) | data formatting | bytes 4718592 | tf_op jit(solution)/shard_map/reshape | solution.py:78
  206.9 0.0 copy-start.6
  206.9 0.0 copy-start.8
  206.9 5.4 %all-to-all-start.3 = ((bf16[2,64,6,1536]{3,0,2,1:T(2,128)(2,1)}), bf16[2,64,6,1536]{3,0,2,1:T(2,128)(2,1)S(1)}, u32[]{:S(2)}, u32[]{:S(2)}) async-start(bf16[2,64,6,1536]{3,0,2,1:T(2,128)(2,1)} %copy.40), calls=%async_computation.3 | async-start | bytes 4718592 | tf_op jit(solution)/shard_map/all_to_all | solution.py:77
  212.3 29.7 %all-to-all-done.3 = bf16[2,64,6,1536]{3,0,2,1:T(2,128)(2,1)S(1)} async-done(((bf16[2,64,6,1536]{3,0,2,1:T(2,128)(2,1)}), bf16[2,64,6,1536]{3,0,2,1:T(2,128)(2,1)S(1)}, u32[]{:S(2)}, u32[]{:S(2)}) %all-to-all-start.3) | async-done | bytes 2359328 | tf_op jit(solution)/shard_map/all_to_all | solution.py:77
  242.0 0.0 copy-done.4
  242.0 0.0 copy-done.6
  242.0 0.0 copy-done.8
  242.0 1.3 fusion.39
  (3 shorter events, 0.0 us)
Async XLA Ops:
  0.8 1.3 copy-start.1
  82.7 39.0 %copy-start = (bf16[2,64,1536]{2,1,0:T(8,128)(2,1)S(1)}, bf16[2,64,1536]{2,1,0:T(8,128)(2,1)}, u32[]{:S(2)}) copy-start(bf16[2,64,1536]{2,1,0:T(8,128)(2,1)} %param.6) | copy-start | bytes 1179652
  86.5 5.7 %copy-start.2 = (s32[1,2,64,4]{3,2,1,0:T(8,128)S(1)}, s32[1,2,64,4]{3,2,1,0:T(8,128)}, u32[]{:S(2)}) copy-start(s32[1,2,64,4]{3,2,1,0:T(8,128)} %copy-done.1) | copy-start | bytes 6148
  86.5 35.1 %all-to-all-start.1 = ((bf16[2,64,6,1536]{3,0,2,1:T(2,128)(2,1)}), bf16[2,64,6,1536]{3,0,2,1:T(2,128)(2,1)S(1)}, u32[]{:S(2)}, u32[]{:S(2)}) async-start(bf16[2,64,6,1536]{3,0,2,1:T(2,128)(2,1)} %copy.36), calls=%async_computation.1 | async-start | bytes 4718592 | tf_op jit(solution)/shard_map/all_to_all | solution.py:77
  92.5 36.7 %copy-start.7 = (pred[2,64,384]{2,1,0:T(8,128)(4,1)}, pred[2,64,384]{2,1,0:T(8,128)(4,1)S(1)}, u32[]{:S(2)}) copy-start(pred[2,64,384]{2,1,0:T(8,128)(4,1)S(1)} %fusion.46) | copy-start | bytes 147460
  122.2 7.0 %copy-start.3 = (bf16[2,64,1536]{2,1,0:T(8,128)(2,1)}, bf16[2,64,1536]{2,1,0:T(8,128)(2,1)S(1)}, u32[]{:S(2)}) copy-start(bf16[2,64,1536]{2,1,0:T(8,128)(2,1)S(1)} %fusion.34) | copy-start | bytes 1179652
  122.2 7.0 %collective-permute-start = (bf16[2,64,1536]{2,1,0:T(8,128)(2,1)S(1)}, bf16[2,64,1536]{2,1,0:T(8,128)(2,1)S(1)}, u32[]{:S(2)}, u32[]{:S(2)}) collective-permute-start(bf16[2,64,1536]{2,1,0:T(8,128)(2,1)S(1)} %fusion.34), channel_id=1, source_target_pairs={{64,0},{65,1},{66,2},{67,3},{68,4},{69,5},{70,6},{71,7},{72,8},{73... | collective-permute-start | bytes 1179656 | tf_op jit(solution)/shard_map/ppermute | solution.py:12
  129.2 0.8 copy-start.5
  203.1 38.9 %copy-start.4 = (bf16[2,64,1536]{2,1,0:T(8,128)(2,1)S(1)}, bf16[2,64,1536]{2,1,0:T(8,128)(2,1)}, u32[]{:S(2)}) copy-start(bf16[2,64,1536]{2,1,0:T(8,128)(2,1)} %copy-done.3) | copy-start | bytes 1179652
  206.9 35.1 %copy-start.6 = (bf16[2,64,1536]{2,1,0:T(8,128)(2,1)S(1)}, bf16[2,64,1536]{2,1,0:T(8,128)(2,1)}, u32[]{:S(2)}) copy-start(bf16[2,64,1536]{2,1,0:T(8,128)(2,1)} %copy-done.5) | copy-start | bytes 1179652
  206.9 35.1 %copy-start.8 = (pred[2,64,384]{2,1,0:T(8,128)(4,1)S(1)}, pred[2,64,384]{2,1,0:T(8,128)(4,1)}, u32[]{:S(2)}) copy-start(pred[2,64,384]{2,1,0:T(8,128)(4,1)} %copy-done.7) | copy-start | bytes 147460
  206.9 35.1 %all-to-all-start.3 = ((bf16[2,64,6,1536]{3,0,2,1:T(2,128)(2,1)}), bf16[2,64,6,1536]{3,0,2,1:T(2,128)(2,1)S(1)}, u32[]{:S(2)}, u32[]{:S(2)}) async-start(bf16[2,64,6,1536]{3,0,2,1:T(2,128)(2,1)} %copy.40), calls=%async_computation.3 | async-start | bytes 4718592 | tf_op jit(solution)/shard_map/all_to_all | solution.py:77
where the time goes:
time: 246 us; the launch traced here: 243 us
  blocking collectives  80.6 us (33%)
  waiting for transfers between devices  59.9 us (24%)
  matrix products  46.3 us (19%)
  local copies, waits for them, and re-layouts  39.3 us (16%)
  starting transfers between devices  16.8 us (7%)
    all_to_all x2, blocking collectives, layer_grads(): lax.all_to_all(outgoing.reshape(micro_count, device_count, capacity, mode...  80.6 us
    all_to_all x2, waiting for transfers between devices, layer_grads(): lax.all_to_all(answers.reshape(micro_count, device_count, capacity, model...  58.9 us
    dot_general x2, matrix products, expert_rows(): lax.dot_general(joined, w_gate_up, (((1,), (1,)), ((), ())), preferred_el...  22.2 us
    dot_general x2, matrix products, expert_rows(): lax.dot_general(grad_rows, w_down, (((1,), (1,)), ((), ())), preferred_el...  20.2 us
    reshape x4, local copies, waits for them, and re-layouts, layer_grads(): answers.reshape(micro_count, device_count, capacity, model_width)  14.7 us
    mul x5, local copies, waits for them, and re-layouts, layer_grads(): pick_weights[..., None] * incoming[:, :, None, :].astype(jnp.float32)  11.6 us
    all_to_all x2, starting transfers between devices, layer_grads(): lax.all_to_all(answers.reshape(micro_count, device_count, capacity, model...  10.9 us
    ppermute x1, starting transfers between devices, passed_along(): lax.ppermute(value, axis, [(source, source + steps) for source in range(i...  5.91 us
  transfers between devices with their start and end apart: 3, of which 3 were waited for; matrix products, arithmetic and copies ran while one was open for 0% of the time, Pallas kernels for 0%

commit v1 on v0

v1 whole, which is shorter than its diff:
```python
import jax
import jax.numpy as jnp
from jax import lax
from jax.experimental import pallas as pl
from jax.experimental.pallas import tpu as pltpu
from jax.sharding import PartitionSpec as P

alpha_glu = 1.702
BF = jnp.bfloat16
F32 = jnp.float32

MODEL = 1536
HIDDEN = 1536
TOKENS = 64
EXPERTS = 64
TOP = 4
CAP = 6
SLOTS = EXPERTS * CAP
PACK = 8
PART = MODEL // 4
WIDE = 3 * PART
ROWS = EXPERTS * PACK
BLOCKS = 16
GROUP_SLOTS = BLOCKS * CAP
GROUP_ROWS = BLOCKS * PACK
GROUPS = EXPERTS // BLOCKS
TILE = 256
STEPS = HIDDEN // TILE
BIG = 48 * 1024 * 1024


def iota(shape, axis):
    return lax.broadcasted_iota(jnp.int32, shape, axis)


def dot(a, b, contract=((1,), (0,))):
    return lax.dot_general(a, b, (contract, ((), ())), preferred_element_type=F32)


def chosen_meta(layer, own_ref, got_ref):
    section = lax.axis_index("section")
    own = own_ref[:, pl.ds(section, 1)]
    got = got_ref[:, pl.ds(section, 1)]
    both = jnp.where(section == layer, own, got)
    return both[0, 0], both[1, 0]


def named(ids, shape):
    expert = (iota(shape, 0) // PACK).astype(F32)
    return [ids[k : k + 1, :] == expert for k in range(TOP)]


def slot_counts(picked, lanes):
    earlier = (iota((TOKENS, lanes), 0) < (iota((TOKENS, lanes), 1) % TOKENS)).astype(BF)
    return dot(picked.astype(BF), earlier)


def wanted_slots(shape, part):
    row = iota(shape, 0) % PACK
    main = row
    extra = jnp.where(row >= CAP, 3 * (row - CAP) + part, -1)
    return main, extra


def send_masks(ids, weights):
    shape = (ROWS, 4 * TOKENS)
    hits = named(ids, shape)
    weight = jnp.zeros(shape, F32)
    for k in range(TOP):
        weight = weight + jnp.where(hits[k], weights[k : k + 1, :], 0.0)
    picked = hits[0] | hits[1] | hits[2] | hits[3]
    counts = slot_counts(jnp.where(picked, 1.0, 0.0)[:, :TOKENS], 4 * TOKENS)
    counts = jnp.where(picked, counts, -2.0)
    lead = weight.astype(BF).astype(F32)
    group = iota(shape, 1) // TOKENS
    value = jnp.where(group < 2, lead, weight - lead)
    masks = []
    for part in range(3):
        main, extra = wanted_slots(shape, part)
        slot = jnp.where(group % 2 == 0, main, extra).astype(F32)
        masks.append(jnp.where(counts == slot, value, 0.0).astype(BF))
    return masks


def gather_masks(ids):
    shape = (ROWS, 2 * TOKENS)
    hits = named(ids, shape)
    picked = hits[0] | hits[1] | hits[2] | hits[3]
    counts = slot_counts(jnp.where(picked, 1.0, 0.0)[:, :TOKENS], 2 * TOKENS)
    counts = jnp.where(picked, counts, -2.0)
    group = iota(shape, 1) // TOKENS
    masks = []
    for part in range(3):
        main, extra = wanted_slots(shape, part)
        slot = jnp.where(group == 0, main, extra).astype(F32)
        masks.append(jnp.where(counts == slot, 1.0, 0.0))
    return masks


def send_rows(masks, grads, out_ref):
    last = grads[:, WIDE:]
    for part in range(3):
        here = grads[:, part * PART : (part + 1) * PART]
        rows = jnp.concatenate([here, last, here, last], axis=0)
        out_ref[:, part * PART : (part + 1) * PART] = dot(masks[part], rows).astype(BF)


def gather_rows(masks_ref, packed_ref, grads):
    pieces = []
    last = jnp.zeros((TOKENS, PART), F32)
    for part in range(3):
        both = dot(masks_ref[part], packed_ref[:, part * PART : (part + 1) * PART])
        pieces.append(both[:TOKENS])
        last = last + both[TOKENS:]
    total = jnp.concatenate(pieces + [last], axis=1)
    return (grads.astype(F32) + total).astype(BF)


def first_kernel(own_ref, got_ref, grads_ref, out_ref):
    ids, weights = chosen_meta(1, own_ref, got_ref)
    section = lax.axis_index("section")
    send_rows(send_masks(ids, weights), grads_ref[section], out_ref)


def routes_kernel(own_ref, got_ref, send_ref, gather_one_ref, gather_zero_ref):
    ids, _ = chosen_meta(1, own_ref, got_ref)
    for part, mask in enumerate(gather_masks(ids[:, : 2 * TOKENS])):
        gather_one_ref[part] = mask.T.astype(BF)
    ids, weights = chosen_meta(0, own_ref, got_ref)
    for part, mask in enumerate(gather_masks(ids[:, : 2 * TOKENS])):
        gather_zero_ref[part] = mask.T.astype(BF)
    for part, mask in enumerate(send_masks(ids, weights)):
        send_ref[part] = mask


def relay_kernel(packed_ref, gather_ref, send_ref, grads_ref, lower_ref, out_ref):
    section = lax.axis_index("section")
    lower = gather_rows(gather_ref, packed_ref, grads_ref[section])
    lower_ref[...] = lower
    send_rows([send_ref[part] for part in range(3)], lower, out_ref)


def last_kernel(packed_ref, gather_ref, grads_ref, out_ref):
    out_ref[...] = gather_rows(gather_ref, packed_ref, grads_ref[...])


def group_masks():
    shape = (GROUP_ROWS, GROUP_SLOTS)
    row, column = iota(shape, 0), iota(shape, 1)
    block = (column * 43) >> 8
    slot = column - CAP * block
    same = (row >> 3) == block
    inner = row & 7
    main = same & (inner == slot)
    extra = [same & (inner >= CAP) & (slot == 3 * (inner - CAP) + part) for part in range(3)]
    return [jnp.where(mask, 1.0, 0.0) for mask in [main] + extra]


def expert_kernel(
    layer, packed_ref, own_pre, got_pre, own_down, got_down, own_up, got_up,
    out_ref, pre, down, up, rows, joined, answers, sems,
):
    section = lax.axis_index("section")

    def copies(from_pre, from_down, from_up):
        made = []
        for step in range(STEPS):
            here = pl.ds(step * TILE, TILE)
            there = pl.ds(HIDDEN + step * TILE, TILE)
            made.append(pltpu.make_async_copy(from_down.at[here], down.at[here], sems.at[0, step]))
            made.append(pltpu.make_async_copy(from_pre.at[:, here], pre.at[:, here], sems.at[1, step]))
            made.append(pltpu.make_async_copy(from_pre.at[:, there], pre.at[:, there], sems.at[2, step]))
        for step in range(STEPS):
            here = pl.ds(step * TILE, TILE)
            made.append(pltpu.make_async_copy(from_up.at[here], up.at[here], sems.at[3, step]))
        return made

    @pl.when(section == layer)
    def _():
        for copy in copies(own_pre.at[layer], own_down, own_up):
            copy.start()

    @pl.when(section != layer)
    def _():
        for copy in copies(got_pre, got_down, got_up):
            copy.start()

    waits = copies(got_pre, got_down, got_up)
    masks = group_masks()
    pack_masks = [
        jnp.concatenate([masks[0], masks[1 + part]], axis=1).astype(BF) for part in range(3)
    ]
    open_main = masks[0].T.astype(BF)
    open_last = jnp.concatenate([masks[1 + part].T for part in range(3)], axis=1).astype(BF)
    for group in range(GROUPS):
        taken = packed_ref[group * GROUP_ROWS : (group + 1) * GROUP_ROWS, :]
        target = slice(group * GROUP_SLOTS, (group + 1) * GROUP_SLOTS)
        rows[target, :WIDE] = dot(open_main, taken).astype(BF)
        stacked = jnp.concatenate(
            [taken[:, part * PART : (part + 1) * PART] for part in range(3)], axis=0
        )
        rows[target, WIDE:] = dot(open_last, stacked).astype(BF)

    for step in range(STEPS):
        here = slice(step * TILE, (step + 1) * TILE)
        there = slice(HIDDEN + step * TILE, HIDDEN + (step + 1) * TILE)
        for copy in waits[3 * step : 3 * step + 3]:
            copy.wait()
        back = dot(rows[...], down[here, :], ((1,), (1,)))
        gate = pre[:, here].astype(F32)
        linear = pre[:, there].astype(F32)
        sigmoid = jax.nn.sigmoid(alpha_glu * gate)
        joined[:, there] = (back * gate * sigmoid).astype(BF)
        joined[:, here] = (
            back * (linear + 1.0) * sigmoid * (1.0 + alpha_glu * gate * (1.0 - sigmoid))
        ).astype(BF)
    for step in range(STEPS):
        here = slice(step * TILE, (step + 1) * TILE)
        waits[3 * STEPS + step].wait()
        answers[:, here] = dot(joined[...], up[here, :], ((1,), (1,))).astype(BF)
    for group in range(GROUPS):
        source = slice(group * GROUP_SLOTS, (group + 1) * GROUP_SLOTS)
        target = slice(group * GROUP_ROWS, (group + 1) * GROUP_ROWS)
        last = answers[source, WIDE:]
        for part in range(3):
            columns = slice(part * PART, (part + 1) * PART)
            both = jnp.concatenate([answers[source, columns], last], axis=0)
            out_ref[target, columns] = dot(pack_masks[part], both).astype(BF)


def shape(*dims, dtype=BF):
    return jax.ShapeDtypeStruct(dims, dtype)


def small_call(kernel, outs, name, flops):
    return pl.pallas_call(
        kernel,
        out_shape=outs,
        name=name,
        compiler_params=pltpu.CompilerParams(vmem_limit_bytes=24 * 1024 * 1024),
        cost_estimate=pl.CostEstimate(flops=flops, bytes_accessed=4_000_000, transcendentals=0),
    )


def expert_call(layer):
    whole = pl.BlockSpec(memory_space=pltpu.VMEM)
    far = pl.BlockSpec(memory_space=pl.ANY)
    return pl.pallas_call(
        lambda *refs: expert_kernel(layer, *refs),
        out_shape=shape(ROWS, WIDE),
        in_specs=[whole] + [far] * 6,
        out_specs=whole,
        name=f"expert_layer_{layer}",
        scratch_shapes=[
            pltpu.VMEM((SLOTS, 2 * HIDDEN), BF),
            pltpu.VMEM((HIDDEN, MODEL), BF),
            pltpu.VMEM((MODEL, 2 * HIDDEN), BF),
            pltpu.VMEM((SLOTS, MODEL), BF),
            pltpu.VMEM((SLOTS, 2 * HIDDEN), BF),
            pltpu.VMEM((SLOTS, MODEL), BF),
            pltpu.SemaphoreType.DMA((4, STEPS)),
        ],
        compiler_params=pltpu.CompilerParams(vmem_limit_bytes=BIG),
        cost_estimate=pl.CostEstimate(
            flops=6 * SLOTS * MODEL * HIDDEN, bytes_accessed=20_000_000, transcendentals=0
        ),
    )


def exchange(packed):
    return lax.all_to_all(
        packed.reshape(EXPERTS, PACK, WIDE), "ep", split_axis=0, concat_axis=0, tiled=True
    ).reshape(ROWS, WIDE)


def swapped(value):
    return lax.ppermute(value, "section", [(0, 1), (1, 0)])


def body(top_grads, expert_ids, route_weights, preacts, w_gate_up, w_down):
    section = lax.axis_index("section")
    ids = expert_ids[0].transpose(0, 2, 1).astype(F32)
    weights = route_weights[0].transpose(0, 2, 1)
    own_meta = jnp.tile(jnp.stack([ids, weights]), (1, 1, 1, 4))
    got_meta = swapped(own_meta)
    own_pre = preacts[0, :, 0]
    own_down, own_up = w_down[0, 0], w_gate_up[0, 0]
    got_down = swapped(own_down)
    got_pre = swapped(lax.dynamic_index_in_dim(own_pre, 1 - section, 0, keepdims=False))
    got_up = swapped(own_up)

    packed = small_call(first_kernel, shape(ROWS, WIDE), "send_first", 300_000_000)(
        own_meta, got_meta, top_grads
    )
    send_zero, gather_one, gather_zero = small_call(
        routes_kernel,
        [shape(3, ROWS, 4 * TOKENS), shape(3, 2 * TOKENS, ROWS), shape(3, 2 * TOKENS, ROWS)],
        "routes",
        1_000_000_000,
    )(own_meta, got_meta)
    arrived = exchange(packed)
    operands = (own_pre, got_pre, own_down, got_down, own_up, got_up)
    answered = expert_call(1)(arrived, *operands)
    returned = exchange(answered)
    lower, packed = small_call(
        relay_kernel, [shape(TOKENS, MODEL), shape(ROWS, WIDE)], "relay", 500_000_000
    )(returned, gather_one, send_zero, top_grads)
    from_zero = lax.ppermute(lower, "section", [(0, 1)])
    arrived = exchange(packed)
    answered = expert_call(0)(arrived, *operands)
    returned = exchange(answered)
    final = small_call(last_kernel, shape(TOKENS, MODEL), "gather_last", 200_000_000)(
        returned, gather_zero, lower
    )
    from_one = lax.ppermute(final, "section", [(1, 0)])
    first = jnp.where(section == 0, final, from_zero)
    second = jnp.where(section == 0, from_one, lower)
    return jnp.stack([first, second])[None]


def solution(mesh):
    placed = (
        P(None, "ep", None),
        P("section", None, "ep", None),
        P("section", None, "ep", None),
        P("section", None, "ep", None, None),
        P("section", "ep", None, None),
        P("section", "ep", None, None),
    )
    return jax.shard_map(
        body, mesh=mesh, in_specs=placed, out_specs=P("section", None, "ep", None), check_vma=False
    )
```

time: 246 us -> 161 us (0.65)
  matrix products: 46.3 us -> 0 us
  Pallas kernels: 0 us -> 36.3 us
  local copies, waits for them, and re-layouts: 39.3 us -> 9.64 us
  blocking collectives: 80.6 us -> 53 us
  waiting for transfers between devices: 59.9 us -> 40.9 us
  starting transfers between devices: 16.8 us -> 19.8 us
    dot_general x9 -> x0, matrix products: 46.3 us -> none  [the longest x2 22.2 us: expert_rows(): lax.dot_general(joined, w_gate_up, (((1,), (1,)), ((), ())), preferred_el...]
    pallas_call x0 -> x6, Pallas kernels: none -> 36.3 us  [the longest x1 16.5 us: body(): answered = expert_call(1)(arrived, *operands)]
    all_to_all x2, waiting for transfers between devices: 58.9 us -> 29.5 us  [exchange(): lax.all_to_all(packed.reshape(EXPERTS, PACK, WIDE), 'ep', split_axis=0, c...]
    all_to_all x2, blocking collectives: 80.6 us -> 53 us  [exchange(): lax.all_to_all(packed.reshape(EXPERTS, PACK, WIDE), 'ep', split_axis=0, c...]
    reshape x6 -> x0, local copies, waits for them, and re-layouts: 19.2 us -> none  [the longest x4 14.7 us: layer_grads(): answers.reshape(micro_count, device_count, capacity, model_width)]
    mul x5 -> x0, local copies, waits for them, and re-layouts: 11.6 us -> none  [layer_grads(): pick_weights[..., None] * incoming[:, :, None, :].astype(jnp.float32)]
    ppermute x1 -> x6, waiting for transfers between devices: 1.09 us -> 11.4 us  [the longest x4 10.4 us: swapped(): return lax.ppermute(value, 'section', [(0, 1), (1, 0)])]
    convert_element_type x3 -> x0, local copies, waits for them, and re-layouts: 4.96 us -> none  [the longest x2 4.85 us: layer_grads(): outgoing = jnp.einsum('mps,mpd->msd', slot_hot, scaled, preferred_element...]
  transfers between devices with their start and end apart: 3 -> 8, of which waited for: 3 -> 4; matrix products, arithmetic and copies ran while one was open for 0% -> 2% of each run, Pallas kernels for 0% -> 2%
where the time goes in v1:
time: 161 us
  blocking collectives  53 us (33%)
  waiting for transfers between devices  40.9 us (25%)
  Pallas kernels  36.3 us (23%)
  starting transfers between devices  19.8 us (12%)
  local copies, waits for them, and re-layouts  9.64 us (6%)
    all_to_all x2, blocking collectives, exchange(): lax.all_to_all(packed.reshape(EXPERTS, PACK, WIDE), 'ep', split_axis=0, c...  53 us
    all_to_all x2, waiting for transfers between devices, exchange(): lax.all_to_all(packed.reshape(EXPERTS, PACK, WIDE), 'ep', split_axis=0, c...  29.5 us
    pallas_call x1, Pallas kernels, body(): answered = expert_call(1)(arrived, *operands)  16.5 us
    pallas_call x1, Pallas kernels, body(): answered = expert_call(0)(arrived, *operands)  16.4 us
    all_to_all x2, starting transfers between devices, exchange(): lax.all_to_all(packed.reshape(EXPERTS, PACK, WIDE), 'ep', split_axis=0, c...  11.1 us
    ppermute x4, waiting for transfers between devices, swapped(): return lax.ppermute(value, 'section', [(0, 1), (1, 0)])  10.4 us
    unnamed x28, local copies, waits for them, and re-layouts  6.29 us
    ppermute x1, starting transfers between devices, body(): from_one = lax.ppermute(final, 'section', [(1, 0)])  5.46 us
  transfers between devices with their start and end apart: 8, of which 4 were waited for; matrix products, arithmetic and copies ran while one was open for 2% of the time, Pallas kernels for 2%

profile of v1, /device:TPU:1, one launch (start us, length us, event | category | flops | bytes accessed | tf_op | source)
XLA Modules:
  0.0 160.7 jit_solution(12362990706409727293)
XLA Ops:
  0.0 1.4 collective-permute-start.3
  1.4 0.0 collective-permute-start.2
  1.4 0.0 copy-start.12
  1.4 0.0 copy-start.13
  1.4 0.0 copy-start
  1.4 3.3 %dynamic-slice_bitcast_fusion = bf16[384,3072]{1,0:T(8,128)(2,1)} fusion(bf16[1,2,1,384,3072]{4,3,2,1,0:T(8,128)(2,1)} %param.9, s32[]{:T(128)S(6)} %select_n.17), kind=kLoop, calls=%fused_computation | loop fusion | bytes 4718596 | tf_op jit(solution)/shard_map/jit(dynamic_index_in_dim)/squeeze | solution.py:289
  4.7 0.5 collective-permute-start.1
  5.2 0.0 copy-done.12
  5.2 0.0 copy-done.13
  5.2 0.1 tile.10.own_ref
  5.3 0.0 collective-permute-start
  5.4 10.4 %collective-permute-done.got_ref = f32[2,2,4,256]{3,2,1,0:T(4,128)S(1)} collective-permute-done((f32[2,2,4,256]{3,2,1,0:T(4,128)S(1)}, f32[2,2,4,256]{3,2,1,0:T(4,128)S(1)}, u32[]{:S(2)}, u32[]{:S(2)}) %collective-permute-start) | collective-permute-done | bytes 16416 | tf_op jit(solution)/shard_map/ppermute | solution.py:277
  15.8 0.0 copy-done
  15.8 0.0 copy-start.10
  15.8 0.9 send_first.1
  16.7 29.8 %all_to_all.20 = bf16[64,8,1152]{2,1,0:T(8,128)(2,1)S(1)} all-to-all(bf16[64,8,1152]{2,1,0:T(8,128)(2,1)S(1)} %bitcast.32), channel_id=1, replica_groups=mesh['section'=2,'ep'=64] {'ep'}, dimensions={0} | all-to-all | bytes 2359296 | tf_op jit(solution)/shard_map/all_to_all | solution.py:271
  46.5 0.0 collective-permute-done.1.refs_2_
  46.6 0.0 copy-done.10
  46.6 0.0 collective-permute-done.2.refs_4_
  46.6 0.0 collective-permute-done.3.refs_6_
  46.6 16.5 %expert_layer_1.1 = bf16[512,1152]{1,0:T(8,128)(2,1)} custom-call(bf16[512,1152]{1,0:T(8,128)(2,1)S(1)} %bitcast.30, bf16[2,384,3072]{2,1,0:T(8,128)(2,1)} %bitcast.39, bf16[384,3072]{1,0:T(8,128)(2,1)S(1)} %collective-permute-done.1.refs_2_, bf16[1536,1536]{1,0:T(8,128)(2,1)} %bitcast.42, bf16[1536,1536]{1,0:T(8,128)(2,1)} %collective-permute-done.2.refs_4_, ...), custom_call_target="tpu_custom_call" | custom-call | flops 5435817984 | bytes 20000000 | tf_op jit(solution)/shard_map/expert_layer_1/pallas_call | solution.py:303
  63.1 5.1 %all-to-all-start.1 = ((bf16[64,8,1152]{2,1,0:T(8,128)(2,1)}), bf16[64,8,1152]{2,1,0:T(8,128)(2,1)S(1)}, u32[]{:S(2)}, u32[]{:S(2)}) async-start(bf16[64,8,1152]{2,1,0:T(8,128)(2,1)} %bitcast.12), calls=%async_computation.1 | async-start | bytes 2359296 | tf_op jit(solution)/shard_map/all_to_all | solution.py:271
  68.2 0.0 copy-start.11
  68.2 0.7 copy-done.11
  68.9 1.2 routes.1
  70.1 0.0 copy-start.2
  70.1 0.9 copy-done.2
  71.0 0.0 copy-start.6
  71.0 0.8 copy-done.6
  71.8 0.0 copy-start.8
  71.8 0.7 copy-done.8
  72.5 13.3 %all-to-all-done.1 = bf16[64,8,1152]{2,1,0:T(8,128)(2,1)S(1)} async-done(((bf16[64,8,1152]{2,1,0:T(8,128)(2,1)}), bf16[64,8,1152]{2,1,0:T(8,128)(2,1)S(1)}, u32[]{:S(2)}, u32[]{:S(2)}) %all-to-all-start.1) | async-done | bytes 1179680 | tf_op jit(solution)/shard_map/all_to_all | solution.py:271
  85.9 0.0 copy-start.1
  85.9 1.0 copy-done.1
  86.9 0.0 copy-start.3
  86.9 1.1 copy-done.3
  88.0 0.0 copy-start.9
  88.0 1.0 copy-done.9
  89.0 0.9 relay.1
  89.9 0.0 copy-start.4
  89.9 23.1 %all_to_all.21 = bf16[64,8,1152]{2,1,0:T(8,128)(2,1)S(1)} all-to-all(bf16[64,8,1152]{2,1,0:T(8,128)(2,1)S(1)} %bitcast.35), channel_id=1, replica_groups=mesh['section'=2,'ep'=64] {'ep'}, dimensions={0} | all-to-all | bytes 2359296 | tf_op jit(solution)/shard_map/all_to_all | solution.py:271
  113.1 0.0 copy-done.4
  113.1 16.4 %expert_layer_0.1 = bf16[512,1152]{1,0:T(8,128)(2,1)} custom-call(bf16[512,1152]{1,0:T(8,128)(2,1)S(1)} %bitcast.31, bf16[2,384,3072]{2,1,0:T(8,128)(2,1)} %bitcast.40, bf16[384,3072]{1,0:T(8,128)(2,1)S(1)} %collective-permute-done.1.refs_2_, bf16[1536,1536]{1,0:T(8,128)(2,1)} %bitcast.43, bf16[1536,1536]{1,0:T(8,128)(2,1)} %collective-permute-done.2.refs_4_, ...), custom_call_target="tpu_custom_call" | custom-call | flops 5435817984 | bytes 20000000 | tf_op jit(solution)/shard_map/expert_layer_0/pallas_call | solution.py:310
  129.5 0.0 copy-start.5
  129.5 0.0 copy-start.7
  129.5 6.0 %all-to-all-start.3 = ((bf16[64,8,1152]{2,1,0:T(8,128)(2,1)}), bf16[64,8,1152]{2,1,0:T(8,128)(2,1)S(1)}, u32[]{:S(2)}, u32[]{:S(2)}) async-start(bf16[64,8,1152]{2,1,0:T(8,128)(2,1)} %bitcast.16), calls=%async_computation.3 | async-start | bytes 2359296 | tf_op jit(solution)/shard_map/all_to_all | solution.py:271
  135.5 0.0 copy-done.5
  135.5 1.3 collective-permute-start.4
  136.8 16.2 %all-to-all-done.3 = bf16[64,8,1152]{2,1,0:T(8,128)(2,1)S(1)} async-done(((bf16[64,8,1152]{2,1,0:T(8,128)(2,1)}), bf16[64,8,1152]{2,1,0:T(8,128)(2,1)S(1)}, u32[]{:S(2)}, u32[]{:S(2)}) %all-to-all-start.3) | async-done | bytes 1179680 | tf_op jit(solution)/shard_map/all_to_all | solution.py:271
  153.0 0.0 copy-done.7
  153.0 0.4 gather_last.1
  153.3 5.5 %collective-permute-start.5 = (bf16[64,1536]{1,0:T(8,128)(2,1)S(1)}, bf16[64,1536]{1,0:T(8,128)(2,1)S(1)}, u32[]{:S(2)}, u32[]{:S(2)}) collective-permute-start(bf16[64,1536]{1,0:T(8,128)(2,1)S(1)} %gather_last.1), channel_id=1, source_target_pairs={{64,0},{65,1},{66,2},{67,3},{68,4},{69,5},{70,6},{71,7},{72,8},{73... | collective-permute-start | bytes 589832 | tf_op jit(solution)/shard_map/ppermute | solution.py:315
  158.8 0.0 collective-permute-done.4
  158.8 1.0 collective-permute-done.5
  159.9 0.8 maximum_bitcast_fusion
  (5 shorter events, 0.1 us)
Async XLA Ops:
  0.0 46.6 %collective-permute-start.3 = (bf16[1536,3072]{1,0:T(8,128)(2,1)}, bf16[1536,3072]{1,0:T(8,128)(2,1)}, u32[]{:S(2)}, u32[]{:S(2)}) collective-permute-start(bf16[1536,3072]{1,0:T(8,128)(2,1)} %bitcast.36), channel_id=1, source_target_pairs={{0,64},{64,0},{1,65},{65,1},{2,66},{66,2},{3,67},{67,3},{4,68},{68... | collective-permute-start | bytes 28311560 | tf_op jit(solution)/shard_map/ppermute | solution.py:277
  1.4 45.1 %collective-permute-start.2 = (bf16[1536,1536]{1,0:T(8,128)(2,1)}, bf16[1536,1536]{1,0:T(8,128)(2,1)}, u32[]{:S(2)}, u32[]{:S(2)}) collective-permute-start(bf16[1536,1536]{1,0:T(8,128)(2,1)} %bitcast.41), channel_id=1, source_target_pairs={{0,64},{64,0},{1,65},{65,1},{2,66},{66,2},{3,67},{67,3},{4,68},{68... | collective-permute-start | bytes 14155784 | tf_op jit(solution)/shard_map/ppermute | solution.py:277
  1.4 3.8 %copy-start.12 = (s32[1,2,64,4]{2,3,1,0:T(4,128)S(1)}, s32[1,2,64,4]{2,3,1,0:T(4,128)}, u32[]{:S(2)}) copy-start(s32[1,2,64,4]{2,3,1,0:T(4,128)} %param.7) | copy-start | bytes 6148
  1.4 3.8 %copy-start.13 = (f32[1,2,64,4]{2,3,1,0:T(4,128)S(1)}, f32[1,2,64,4]{2,3,1,0:T(4,128)}, u32[]{:S(2)}) copy-start(f32[1,2,64,4]{2,3,1,0:T(4,128)} %param.8) | copy-start | bytes 6148
  1.4 14.3 %copy-start = (bf16[2,64,1536]{2,1,0:T(8,128)(2,1)S(1)}, bf16[2,64,1536]{2,1,0:T(8,128)(2,1)}, u32[]{:S(2)}) copy-start(bf16[2,64,1536]{2,1,0:T(8,128)(2,1)} %grads_ref.3) | copy-start | bytes 1179652
  4.7 41.9 %collective-permute-start.1 = (bf16[384,3072]{1,0:T(8,128)(2,1)}, bf16[384,3072]{1,0:T(8,128)(2,1)S(1)}, u32[]{:S(2)}, u32[]{:S(2)}) collective-permute-start(bf16[384,3072]{1,0:T(8,128)(2,1)} %dynamic-slice_bitcast_fusion), channel_id=1, source_target_pairs={{0,64},{64,0},{1,65},{65,1},{2,66},{66,2},{3,67},{67,3},{4,68},{68... | collective-permute-start | bytes 7077896 | tf_op jit(solution)/shard_map/ppermute | solution.py:277
  5.3 10.5 %collective-permute-start = (f32[2,2,4,256]{3,2,1,0:T(4,128)S(1)}, f32[2,2,4,256]{3,2,1,0:T(4,128)S(1)}, u32[]{:S(2)}, u32[]{:S(2)}) collective-permute-start(f32[2,2,4,256]{3,2,1,0:T(4,128)S(1)} %tile.10.own_ref), channel_id=1, source_target_pairs={{0,64},{64,0},{1,65},{65,1},{2,66},{66,2},{3,67},{67,3},{4,68},{68... | collective-permute-start | bytes 49160 | tf_op jit(solution)/shard_map/ppermute | solution.py:277
  15.8 30.8 %copy-start.10 = (f32[2,2,4,256]{3,2,1,0:T(4,128)}, f32[2,2,4,256]{3,2,1,0:T(4,128)S(1)}, u32[]{:S(2)}) copy-start(f32[2,2,4,256]{3,2,1,0:T(4,128)S(1)} %collective-permute-done.got_ref) | copy-start | bytes 49156
  63.1 22.8 %all-to-all-start.1 = ((bf16[64,8,1152]{2,1,0:T(8,128)(2,1)}), bf16[64,8,1152]{2,1,0:T(8,128)(2,1)S(1)}, u32[]{:S(2)}, u32[]{:S(2)}) async-start(bf16[64,8,1152]{2,1,0:T(8,128)(2,1)} %bitcast.12), calls=%async_computation.1 | async-start | bytes 2359296 | tf_op jit(solution)/shard_map/all_to_all | solution.py:271
  68.2 0.7 copy-start.11
  70.1 0.9 copy-start.2
  71.0 0.8 copy-start.6
  71.8 0.7 copy-start.8
  85.9 1.0 copy-start.1
  86.9 1.1 copy-start.3
  88.0 1.0 copy-start.9
  89.9 23.1 %copy-start.4 = (bf16[64,1536]{1,0:T(8,128)(2,1)}, bf16[64,1536]{1,0:T(8,128)(2,1)S(1)}, u32[]{:S(2)}) copy-start(bf16[64,1536]{1,0:T(8,128)(2,1)S(1)} %get-tuple-element.14.grads_ref) | copy-start | bytes 589828
  129.5 6.0 %copy-start.5 = (bf16[64,1536]{1,0:T(8,128)(2,1)S(1)}, bf16[64,1536]{1,0:T(8,128)(2,1)}, u32[]{:S(2)}) copy-start(bf16[64,1536]{1,0:T(8,128)(2,1)} %copy-done.4) | copy-start | bytes 589828
  129.5 23.5 %copy-start.7 = (bf16[3,128,512]{2,1,0:T(8,128)(2,1)S(1)}, bf16[3,128,512]{2,1,0:T(8,128)(2,1)}, u32[]{:S(2)}) copy-start(bf16[3,128,512]{2,1,0:T(8,128)(2,1)} %copy-done.6) | copy-start | bytes 1179652
  129.5 23.5 %all-to-all-start.3 = ((bf16[64,8,1152]{2,1,0:T(8,128)(2,1)}), bf16[64,8,1152]{2,1,0:T(8,128)(2,1)S(1)}, u32[]{:S(2)}, u32[]{:S(2)}) async-start(bf16[64,8,1152]{2,1,0:T(8,128)(2,1)} %bitcast.16), calls=%async_computation.3 | async-start | bytes 2359296 | tf_op jit(solution)/shard_map/all_to_all | solution.py:271
  135.5 23.3 %collective-permute-start.4 = (bf16[64,1536]{1,0:T(8,128)(2,1)S(1)}, bf16[64,1536]{1,0:T(8,128)(2,1)S(1)}, u32[]{:S(2)}, u32[]{:S(2)}) collective-permute-start(bf16[64,1536]{1,0:T(8,128)(2,1)S(1)} %copy-done.5), channel_id=1, source_target_pairs={{0,64},{1,65},{2,66},{3,67},{4,68},{5,69},{6,70},{7,71},{8,72},{9,... | collective-permute-start | bytes 589832 | tf_op jit(solution)/shard_map/ppermute | solution.py:308
  153.3 6.5 %collective-permute-start.5 = (bf16[64,1536]{1,0:T(8,128)(2,1)S(1)}, bf16[64,1536]{1,0:T(8,128)(2,1)S(1)}, u32[]{:S(2)}, u32[]{:S(2)}) collective-permute-start(bf16[64,1536]{1,0:T(8,128)(2,1)S(1)} %gather_last.1), channel_id=1, source_target_pairs={{64,0},{65,1},{66,2},{67,3},{68,4},{69,5},{70,6},{71,7},{72,8},{73... | collective-permute-start | bytes 589832 | tf_op jit(solution)/shard_map/ppermute | solution.py:315

commit v2 on v1

--- a/solution.py
+++ b/solution.py
@@ -26,7 +26,11 @@
 GROUPS = EXPERTS // BLOCKS
 TILE = 256
 STEPS = HIDDEN // TILE
+FIRST_WAITS = 2
+SECOND_WAITS = 2
+PIECES = 4
 BIG = 48 * 1024 * 1024
+EXPERT_BIG = 48 * 1024 * 1024
 
 
 def iota(shape, axis):
@@ -37,12 +41,28 @@
     return lax.dot_general(a, b, (contract, ((), ())), preferred_element_type=F32)
 
 
-def chosen_meta(layer, own_ref, got_ref):
-    section = lax.axis_index("section")
-    own = own_ref[:, pl.ds(section, 1)]
-    got = got_ref[:, pl.ds(section, 1)]
-    both = jnp.where(section == layer, own, got)
-    return both[0, 0], both[1, 0]
+def fetch(own, got, layer, pairs, sem):
+    section = lax.axis_index("section")
+    held = [to for to, _ in pairs]
+    slots = [slot for _, slot in pairs]
+
+    @pl.when(section == layer)
+    def _():
+        for source, to, slot in zip(own, held, slots):
+            pltpu.make_async_copy(source.at[layer], to, sem.at[slot]).start()
+
+    @pl.when(section != layer)
+    def _():
+        for source, to, slot in zip(got, held, slots):
+            pltpu.make_async_copy(source.at[1 - layer], to, sem.at[slot]).start()
+
+
+def settle(source, to, sem):
+    pltpu.make_async_copy(source, to, sem).wait()
+
+
+def lanes(value, times):
+    return jnp.concatenate([value] * times, axis=1)
 
 
 def named(ids, shape):
@@ -116,32 +136,80 @@
     return (grads.astype(F32) + total).astype(BF)
 
 
-def first_kernel(own_ref, got_ref, grads_ref, out_ref):
-    ids, weights = chosen_meta(1, own_ref, got_ref)
-    section = lax.axis_index("section")
-    send_rows(send_masks(ids, weights), grads_ref[section], out_ref)
-
-
-def routes_kernel(own_ref, got_ref, send_ref, gather_one_ref, gather_zero_ref):
-    ids, _ = chosen_meta(1, own_ref, got_ref)
-    for part, mask in enumerate(gather_masks(ids[:, : 2 * TOKENS])):
-        gather_one_ref[part] = mask.T.astype(BF)
-    ids, weights = chosen_meta(0, own_ref, got_ref)
-    for part, mask in enumerate(gather_masks(ids[:, : 2 * TOKENS])):
-        gather_zero_ref[part] = mask.T.astype(BF)
-    for part, mask in enumerate(send_masks(ids, weights)):
+def first_kernel(own_ids, own_w, got_ids, got_w, grads_ref, out_ref, ids, weights, grads, sem):
+    section = lax.axis_index("section")
+    fetch((own_ids, own_w), (got_ids, got_w), 1, ((ids, 0), (weights, 1)), sem)
+    rows = pltpu.make_async_copy(grads_ref.at[section], grads, sem.at[2])
+    rows.start()
+    settle(own_ids.at[0], ids, sem.at[0])
+    settle(own_w.at[0], weights, sem.at[1])
+    masks = send_masks(lanes(ids[...].astype(F32), 4), lanes(weights[...], 4))
+    rows.wait()
+    send_rows(masks, grads[...], out_ref)
+
+
+def routes_kernel(
+    own_ids, own_w, got_ids, got_w, send_ref, gather_one_ref, gather_zero_ref,
+    ids_one, ids_zero, weights, sem,
+):
+    fetch((own_ids,), (got_ids,), 1, ((ids_one, 0),), sem)
+    fetch((own_ids, own_w), (got_ids, got_w), 0, ((ids_zero, 1), (weights, 2)), sem)
+    settle(own_ids.at[0], ids_one, sem.at[0])
+    settle(own_ids.at[0], ids_zero, sem.at[1])
+    settle(own_w.at[0], weights, sem.at[2])
+    for ids, out in ((ids_one, gather_one_ref), (ids_zero, gather_zero_ref)):
+        for part, mask in enumerate(gather_masks(lanes(ids[...].astype(F32), 2))):
+            out[part] = mask.T.astype(BF)
+    masks = send_masks(lanes(ids_zero[...].astype(F32), 4), lanes(weights[...], 4))
+    for part, mask in enumerate(masks):
         send_ref[part] = mask
 
 
-def relay_kernel(packed_ref, gather_ref, send_ref, grads_ref, lower_ref, out_ref):
-    section = lax.axis_index("section")
-    lower = gather_rows(gather_ref, packed_ref, grads_ref[section])
+def other_kernel(pre_ref, out_ref, held, sems):
+    section = lax.axis_index("section")
+    into, out = [], []
+    for piece in range(PIECES):
+        here = pl.ds(piece * (SLOTS // PIECES), SLOTS // PIECES)
+        into.append(pltpu.make_async_copy(pre_ref.at[1 - section, here], held.at[here], sems.at[0, piece]))
+        out.append(pltpu.make_async_copy(held.at[here], out_ref.at[here], sems.at[1, piece]))
+    for copy in into:
+        copy.start()
+    for piece in range(PIECES):
+        into[piece].wait()
+        out[piece].start()
+    for copy in out:
+        copy.wait()
+
+
+def relay_kernel(
+    packed_ref, gather_ref, send_ref, grads_ref, lower_ref, out_ref, gather, send, grads, sem
+):
+    section = lax.axis_index("section")
+    copies = [
+        pltpu.make_async_copy(gather_ref, gather, sem.at[0]),
+        pltpu.make_async_copy(grads_ref.at[section], grads, sem.at[1]),
+        pltpu.make_async_copy(send_ref, send, sem.at[2]),
+    ]
+    for copy in copies:
+        copy.start()
+    copies[0].wait()
+    copies[1].wait()
+    lower = gather_rows(gather, packed_ref, grads[...])
     lower_ref[...] = lower
-    send_rows([send_ref[part] for part in range(3)], lower, out_ref)
-
-
-def last_kernel(packed_ref, gather_ref, grads_ref, out_ref):
-    out_ref[...] = gather_rows(gather_ref, packed_ref, grads_ref[...])
+    copies[2].wait()
+    send_rows([send[part] for part in range(3)], lower, out_ref)
+
+
+def last_kernel(packed_ref, gather_ref, grads_ref, out_ref, gather, grads, sem):
+    copies = [
+        pltpu.make_async_copy(gather_ref, gather, sem.at[0]),
+        pltpu.make_async_copy(grads_ref, grads, sem.at[1]),
+    ]
+    for copy in copies:
+        copy.start()
+    for copy in copies:
+        copy.wait()
+    out_ref[...] = gather_rows(gather, packed_ref, grads[...])
 
 
 def group_masks():
@@ -162,30 +230,34 @@
 ):
     section = lax.axis_index("section")
 
-    def copies(from_pre, from_down, from_up):
-        made = []
-        for step in range(STEPS):
-            here = pl.ds(step * TILE, TILE)
-            there = pl.ds(HIDDEN + step * TILE, TILE)
-            made.append(pltpu.make_async_copy(from_down.at[here], down.at[here], sems.at[0, step]))
-            made.append(pltpu.make_async_copy(from_pre.at[:, here], pre.at[:, here], sems.at[1, step]))
-            made.append(pltpu.make_async_copy(from_pre.at[:, there], pre.at[:, there], sems.at[2, step]))
-        for step in range(STEPS):
-            here = pl.ds(step * TILE, TILE)
-            made.append(pltpu.make_async_copy(from_up.at[here], up.at[here], sems.at[3, step]))
-        return made
+    def copies(step, from_pre, from_down, from_up):
+        if step >= STEPS:
+            here = pl.ds((step - STEPS) * TILE, TILE)
+            return [pltpu.make_async_copy(from_up.at[here], up.at[here], sems.at[0, step])]
+        here = pl.ds(step * TILE, TILE)
+        there = pl.ds(HIDDEN + step * TILE, TILE)
+        return [
+            pltpu.make_async_copy(from_down.at[here], down.at[here], sems.at[0, step]),
+            pltpu.make_async_copy(from_pre.at[:, here], pre.at[:, here], sems.at[1, step]),
+            pltpu.make_async_copy(from_pre.at[:, there], pre.at[:, there], sems.at[2, step]),
+        ]
 
     @pl.when(section == layer)
     def _():
-        for copy in copies(own_pre.at[layer], own_down, own_up):
-            copy.start()
+        for step in range(2 * STEPS):
+            for copy in copies(step, own_pre.at[layer], own_down, own_up):
+                copy.start()
 
     @pl.when(section != layer)
     def _():
-        for copy in copies(got_pre, got_down, got_up):
-            copy.start()
-
-    waits = copies(got_pre, got_down, got_up)
+        for step in range(2 * STEPS):
+            for copy in copies(step, got_pre, got_down, got_up):
+                copy.start()
+
+    def finish(step):
+        for copy in copies(step, got_pre, got_down, got_up):
+            copy.wait()
+
     masks = group_masks()
     pack_masks = [
         jnp.concatenate([masks[0], masks[1 + part]], axis=1).astype(BF) for part in range(3)
@@ -201,11 +273,11 @@
         )
         rows[target, WIDE:] = dot(open_last, stacked).astype(BF)
 
-    for step in range(STEPS):
-        here = slice(step * TILE, (step + 1) * TILE)
-        there = slice(HIDDEN + step * TILE, HIDDEN + (step + 1) * TILE)
-        for copy in waits[3 * step : 3 * step + 3]:
-            copy.wait()
+    for step in range(0, STEPS, FIRST_WAITS):
+        here = slice(step * TILE, (step + FIRST_WAITS) * TILE)
+        there = slice(HIDDEN + step * TILE, HIDDEN + (step + FIRST_WAITS) * TILE)
+        for ready in range(step, step + FIRST_WAITS):
+            finish(ready)
         back = dot(rows[...], down[here, :], ((1,), (1,)))
         gate = pre[:, here].astype(F32)
         linear = pre[:, there].astype(F32)
@@ -214,9 +286,10 @@
         joined[:, here] = (
             back * (linear + 1.0) * sigmoid * (1.0 + alpha_glu * gate * (1.0 - sigmoid))
         ).astype(BF)
-    for step in range(STEPS):
-        here = slice(step * TILE, (step + 1) * TILE)
-        waits[3 * STEPS + step].wait()
+    for step in range(0, STEPS, SECOND_WAITS):
+        here = slice(step * TILE, (step + SECOND_WAITS) * TILE)
+        for ready in range(step, step + SECOND_WAITS):
+            finish(STEPS + ready)
         answers[:, here] = dot(joined[...], up[here, :], ((1,), (1,))).astype(BF)
     for group in range(GROUPS):
         source = slice(group * GROUP_SLOTS, (group + 1) * GROUP_SLOTS)
@@ -232,24 +305,42 @@
     return jax.ShapeDtypeStruct(dims, dtype)
 
 
-def small_call(kernel, outs, name, flops):
-    return pl.pallas_call(
+NEAR = pl.BlockSpec(memory_space=pltpu.VMEM)
+FAR = pl.BlockSpec(memory_space=pl.ANY)
+MASKS = [(3, ROWS, 4 * TOKENS), (3, 2 * TOKENS, ROWS), (3, 2 * TOKENS, ROWS)]
+
+
+def call_far(ins, call):
+    def run(*operands):
+        kept = [
+            pltpu.with_memory_space_constraint(value, pltpu.MemorySpace.HBM) if spec is FAR else value
+            for value, spec in zip(operands, ins)
+        ]
+        return call(*kept)
+
+    return run
+
+
+def small_call(kernel, outs, ins, scratch, copies, name, flops, out_specs=NEAR, still=False):
+    call = pl.pallas_call(
         kernel,
         out_shape=outs,
+        in_specs=ins,
+        out_specs=out_specs,
         name=name,
-        compiler_params=pltpu.CompilerParams(vmem_limit_bytes=24 * 1024 * 1024),
+        scratch_shapes=scratch + [pltpu.SemaphoreType.DMA(copies)],
+        compiler_params=pltpu.CompilerParams(vmem_limit_bytes=BIG),
         cost_estimate=pl.CostEstimate(flops=flops, bytes_accessed=4_000_000, transcendentals=0),
     )
+    return call_far(ins, call) if still else call
 
 
 def expert_call(layer):
-    whole = pl.BlockSpec(memory_space=pltpu.VMEM)
-    far = pl.BlockSpec(memory_space=pl.ANY)
     return pl.pallas_call(
         lambda *refs: expert_kernel(layer, *refs),
         out_shape=shape(ROWS, WIDE),
-        in_specs=[whole] + [far] * 6,
-        out_specs=whole,
+        in_specs=[NEAR] + [FAR] * 6,
+        out_specs=NEAR,
         name=f"expert_layer_{layer}",
         scratch_shapes=[
             pltpu.VMEM((SLOTS, 2 * HIDDEN), BF),
@@ -258,9 +349,9 @@
             pltpu.VMEM((SLOTS, MODEL), BF),
             pltpu.VMEM((SLOTS, 2 * HIDDEN), BF),
             pltpu.VMEM((SLOTS, MODEL), BF),
-            pltpu.SemaphoreType.DMA((4, STEPS)),
+            pltpu.SemaphoreType.DMA((3, 2 * STEPS)),
         ],
-        compiler_params=pltpu.CompilerParams(vmem_limit_bytes=BIG),
+        compiler_params=pltpu.CompilerParams(vmem_limit_bytes=EXPERT_BIG),
         cost_estimate=pl.CostEstimate(
             flops=6 * SLOTS * MODEL * HIDDEN, bytes_accessed=20_000_000, transcendentals=0
         ),
@@ -277,44 +368,78 @@
     return lax.ppermute(value, "section", [(0, 1), (1, 0)])
 
 
+def after(value, *others):
+    return lax.optimization_barrier((value,) + others)[0]
+
+
 def body(top_grads, expert_ids, route_weights, preacts, w_gate_up, w_down):
     section = lax.axis_index("section")
-    ids = expert_ids[0].transpose(0, 2, 1).astype(F32)
-    weights = route_weights[0].transpose(0, 2, 1)
-    own_meta = jnp.tile(jnp.stack([ids, weights]), (1, 1, 1, 4))
-    got_meta = swapped(own_meta)
+    own_ids = expert_ids[0].transpose(0, 2, 1)
+    own_w = route_weights[0].transpose(0, 2, 1)
     own_pre = preacts[0, :, 0]
     own_down, own_up = w_down[0, 0], w_gate_up[0, 0]
-    got_down = swapped(own_down)
-    got_pre = swapped(lax.dynamic_index_in_dim(own_pre, 1 - section, 0, keepdims=False))
-    got_up = swapped(own_up)
-
-    packed = small_call(first_kernel, shape(ROWS, WIDE), "send_first", 300_000_000)(
-        own_meta, got_meta, top_grads
-    )
+    got_ids, got_w = swapped(own_ids), swapped(own_w)
+    other_pre = small_call(
+        other_kernel,
+        shape(SLOTS, 2 * HIDDEN),
+        [FAR],
+        [pltpu.VMEM((SLOTS, 2 * HIDDEN), BF)],
+        (2, PIECES),
+        "other_pre",
+        1_000_000,
+        FAR,
+    )(own_pre)
+    got_down = swapped(after(own_down, got_ids, got_w))
+    got_up = swapped(after(own_up, got_ids, got_w))
+    got_pre = swapped(other_pre)
+
+    picks = [pltpu.VMEM((TOP, TOKENS), jnp.int32), pltpu.VMEM((TOP, TOKENS), F32)]
+    grads = pltpu.VMEM((TOKENS, MODEL), BF)
+    packed = small_call(
+        first_kernel, shape(ROWS, WIDE), [FAR] * 5, picks + [grads], (3,), "send_first", 300_000_000
+    )(own_ids, own_w, got_ids, got_w, top_grads)
     send_zero, gather_one, gather_zero = small_call(
         routes_kernel,
-        [shape(3, ROWS, 4 * TOKENS), shape(3, 2 * TOKENS, ROWS), shape(3, 2 * TOKENS, ROWS)],
+        [shape(*dims) for dims in MASKS],
+        [FAR] * 4,
+        picks[:1] + picks,
+        (3,),
         "routes",
         1_000_000_000,
-    )(own_meta, got_meta)
+        [NEAR] * 3,
+    )(own_ids, own_w, after(got_ids, packed), got_w)
     arrived = exchange(packed)
     operands = (own_pre, got_pre, own_down, got_down, own_up, got_up)
     answered = expert_call(1)(arrived, *operands)
     returned = exchange(answered)
     lower, packed = small_call(
-        relay_kernel, [shape(TOKENS, MODEL), shape(ROWS, WIDE)], "relay", 500_000_000
+        relay_kernel,
+        [shape(TOKENS, MODEL), shape(ROWS, WIDE)],
+        [NEAR] + [FAR] * 3,
+        [pltpu.VMEM(MASKS[1], BF), pltpu.VMEM(MASKS[0], BF), grads],
+        (3,),
+        "relay",
+        500_000_000,
+        [NEAR] * 2,
+        True,
     )(returned, gather_one, send_zero, top_grads)
-    from_zero = lax.ppermute(lower, "section", [(0, 1)])
     arrived = exchange(packed)
     answered = expert_call(0)(arrived, *operands)
     returned = exchange(answered)
-    final = small_call(last_kernel, shape(TOKENS, MODEL), "gather_last", 200_000_000)(
-        returned, gather_zero, lower
-    )
-    from_one = lax.ppermute(final, "section", [(1, 0)])
-    first = jnp.where(section == 0, final, from_zero)
-    second = jnp.where(section == 0, from_one, lower)
+    final = small_call(
+        last_kernel,
+        shape(TOKENS, MODEL),
+        [NEAR] + [FAR] * 2,
+        [pltpu.VMEM(MASKS[2], BF), grads],
+        (2,),
+        "gather_last",
+        200_000_000,
+        NEAR,
+        True,
+    )(returned, gather_zero, lower)
+    other = swapped(jnp.where(section == 0, lower, final))
+    first = jnp.where(section == 0, final, other)
+    second = jnp.where(section == 0, other, lower)
     return jnp.stack([first, second])[None]
 
 

time: 161 us -> 140 us (0.87)
  waiting for transfers between devices: 40.9 us -> 33.6 us
  Pallas kernels: 36.3 us -> 29.8 us
  local copies, waits for them, and re-layouts: 9.64 us -> 5.32 us
  starting transfers between devices: 19.8 us -> 16.6 us
    ppermute x4 -> x6, waiting for transfers between devices: 10.4 us -> 2.45 us  [swapped(): return lax.ppermute(value, 'section', [(0, 1), (1, 0)])]
    ppermute x2 -> x0, starting transfers between devices: 6.75 us -> none  [the longest x1 5.46 us: body(): from_one = lax.ppermute(final, 'section', [(1, 0)])]
    pallas_call x1, Pallas kernels: 16.4 us -> 10.6 us  [body(): answered = expert_call(0)(arrived, *operands)]
    pallas_call x1, Pallas kernels: 16.5 us -> 10.8 us  [body(): answered = expert_call(1)(arrived, *operands)]
    pallas_call x4 -> x5, Pallas kernels: 3.39 us -> 8.38 us  [the longest x2 3.46 us: run(): return call(*kept)]
    ppermute x4 -> x6, starting transfers between devices: 1.96 us -> 5.82 us  [swapped(): return lax.ppermute(value, 'section', [(0, 1), (1, 0)])]
    squeeze x1 -> x0, local copies, waits for them, and re-layouts: 3.25 us -> none  [body(): lax.dynamic_index_in_dim(own_pre, 1 - section, 0, keepdims=False)]
    all_to_all x2, waiting for transfers between devices: 29.5 us -> 31.2 us  [exchange(): lax.all_to_all(packed.reshape(EXPERTS, PACK, WIDE), 'ep', split_axis=0, c...]
  transfers between devices with their start and end apart: 8 -> 8, of which waited for: 4 -> 5; matrix products, arithmetic and copies ran while one was open for 2% -> 0% of each run, Pallas kernels for 2% -> 4%
where the time goes in v2:
time: 140 us; the launch traced here: 139 us
  blocking collectives  52.8 us (38%)
  waiting for transfers between devices  33.6 us (24%)
  Pallas kernels  29.8 us (21%)
  starting transfers between devices  16.6 us (12%)
  local copies, waits for them, and re-layouts  5.32 us (4%)
    all_to_all x2, blocking collectives, exchange(): lax.all_to_all(packed.reshape(EXPERTS, PACK, WIDE), 'ep', split_axis=0, c...  52.8 us
    all_to_all x2, waiting for transfers between devices, exchange(): lax.all_to_all(packed.reshape(EXPERTS, PACK, WIDE), 'ep', split_axis=0, c...  31.2 us
    pallas_call x1, Pallas kernels, body(): answered = expert_call(1)(arrived, *operands)  10.8 us
    all_to_all x2, starting transfers between devices, exchange(): lax.all_to_all(packed.reshape(EXPERTS, PACK, WIDE), 'ep', split_axis=0, c...  10.8 us
    pallas_call x1, Pallas kernels, body(): answered = expert_call(0)(arrived, *operands)  10.6 us
    ppermute x6, starting transfers between devices, swapped(): return lax.ppermute(value, 'section', [(0, 1), (1, 0)])  5.82 us
    unnamed x18, local copies, waits for them, and re-layouts  5.32 us
    pallas_call x2, Pallas kernels, run(): return call(*kept)  3.46 us
  transfers between devices with their start and end apart: 8, of which 5 were waited for; matrix products, arithmetic and copies ran while one was open for 0% of the time, Pallas kernels for 4%

profile of v2, /device:TPU:1, one launch (start us, length us, event | category | flops | bytes accessed | tf_op | source)
XLA Modules:
  0.0 139.2 jit_solution(7564066379230455536)
XLA Ops:
  0.0 1.4 %collective-permute-start = (s32[2,4,64]{2,1,0:T(4,128)}, s32[2,4,64]{2,1,0:T(4,128)S(1)}, u32[]{:S(2)}, u32[]{:S(2)}) collective-permute-start(s32[2,4,64]{2,1,0:T(4,128)} %bitcast.29), channel_id=1, source_target_pairs={{0,64},{64,0},{1,65},{65,1},{2,66},{66,2},{3,67},{67,3},{4,68},{68... | collective-permute-start | bytes 6152 | tf_op jit(solution)/shard_map/ppermute | solution.py:368
  1.4 0.0 collective-permute-start.1
  1.4 1.0 collective-permute-done.got_ids
  2.5 0.3 collective-permute-done.1.got_w
  2.8 0.2 collective-permute-start.4
  3.0 0.3 collective-permute-start.3
  3.3 0.0 copy-start.2
  3.3 0.0 copy-start.6
  3.3 0.0 copy-start.7
  3.3 1.8 %other_pre.1 = bf16[384,3072]{1,0:T(8,128)(2,1)S(1)} custom-call(bf16[2,384,3072]{2,1,0:T(8,128)(2,1)} %bitcast.35), custom_call_target="tpu_custom_call" | custom-call | flops 1000000 | bytes 4000000 | tf_op jit(solution)/shard_map/other_pre/pallas_call | solution.py:382
  5.2 0.2 collective-permute-start.2
  5.4 0.0 copy-done.2
  5.4 0.0 copy-done.6
  5.4 0.0 copy-done.7
  5.4 1.4 %send_first.1 = bf16[512,1152]{1,0:T(8,128)(2,1)S(1)} custom-call(s32[2,4,64]{2,1,0:T(4,128)S(1)} %bitcast.30, f32[2,4,64]{2,1,0:T(4,128)S(1)} %bitcast.33, s32[2,4,64]{2,1,0:T(4,128)S(1)} %collective-permute-done.got_ids, f32[2,4,64]{2,1,0:T(4,128)S(1)} %collective-permute-done.1.got_w, bf16[2,64,1536]{2,1,0:T(8,128)(2,1)S(1)} %copy-done.2), custom_call_target="tpu_custom_call" | custom-call | flops 300000000 | bytes 4000000 | tf_op jit(solution)/shard_map/send_first/pallas_call | solution.py:398
  6.9 29.9 %all_to_all.20 = bf16[64,8,1152]{2,1,0:T(8,128)(2,1)S(1)} all-to-all(bf16[64,8,1152]{2,1,0:T(8,128)(2,1)S(1)} %bitcast.25), channel_id=1, replica_groups=mesh['section'=2,'ep'=64] {'ep'}, dimensions={0} | all-to-all | bytes 2359296 | tf_op jit(solution)/shard_map/all_to_all | solution.py:362
  36.7 0.0 collective-permute-done.2.refs_2_
  36.7 0.0 collective-permute-done.3.refs_4_
  36.7 0.0 copy-start.8
  36.7 0.0 collective-permute-done.4.refs_6_
  36.8 2.2 %copy-done.8 = bf16[1536,1536]{1,0:T(8,128)(2,1)} copy-done((bf16[1536,1536]{1,0:T(8,128)(2,1)}, bf16[1536,1536]{1,0:T(8,128)(2,1)S(1)}, u32[]{:S(2)}) %copy-start.8) | copy-done | bytes 4718616
  39.0 10.8 %expert_layer_1.1 = bf16[512,1152]{1,0:T(8,128)(2,1)} custom-call(bf16[512,1152]{1,0:T(8,128)(2,1)S(1)} %bitcast.23, bf16[2,384,3072]{2,1,0:T(8,128)(2,1)} %bitcast.36, bf16[384,3072]{1,0:T(8,128)(2,1)S(1)} %collective-permute-done.2.refs_2_, bf16[1536,1536]{1,0:T(8,128)(2,1)} %bitcast.42, bf16[1536,1536]{1,0:T(8,128)(2,1)} %copy-done.8, ...), custom_call_target="tpu_custom_call" | custom-call | flops 5435817984 | bytes 20000000 | tf_op jit(solution)/shard_map/expert_layer_1/pallas_call | solution.py:413
  49.8 4.9 %all-to-all-start.1 = ((bf16[64,8,1152]{2,1,0:T(8,128)(2,1)}), bf16[64,8,1152]{2,1,0:T(8,128)(2,1)S(1)}, u32[]{:S(2)}, u32[]{:S(2)}) async-start(bf16[64,8,1152]{2,1,0:T(8,128)(2,1)} %bitcast.11), calls=%async_computation.1 | async-start | bytes 2359296 | tf_op jit(solution)/shard_map/all_to_all | solution.py:362
  54.7 1.7 %routes.1 = (bf16[3,512,256]{2,1,0:T(8,128)(2,1)S(1)}, bf16[3,128,512]{2,1,0:T(8,128)(2,1)S(1)}, bf16[3,128,512]{2,1,0:T(8,128)(2,1)S(1)}) custom-call(s32[2,4,64]{2,1,0:T(4,128)S(1)} %bitcast.31, f32[2,4,64]{2,1,0:T(4,128)S(1)} %bitcast.34, s32[2,4,64]{2,1,0:T(4,128)S(1)} %collective-permute-done.got_ids, f32[2,4,64]{2,1,0:T(4,128)S(1)} %collective-permute-done.1.got_w), custom_call_target="tpu_custom_call" | custom-call | flops 1000000000 | bytes 4000000 | tf_op jit(solution)/shard_map/routes/pallas_call | solution.py:401
  56.4 0.0 copy-start.3
  56.4 0.9 copy-done.3
  57.3 0.0 copy-start.4
  57.3 0.8 copy-done.4
  58.1 0.0 copy-start.5
  58.1 0.7 copy-done.5
  58.8 13.7 %all-to-all-done.1 = bf16[64,8,1152]{2,1,0:T(8,128)(2,1)S(1)} async-done(((bf16[64,8,1152]{2,1,0:T(8,128)(2,1)}), bf16[64,8,1152]{2,1,0:T(8,128)(2,1)S(1)}, u32[]{:S(2)}, u32[]{:S(2)}) %all-to-all-start.1) | async-done | bytes 1179680 | tf_op jit(solution)/shard_map/all_to_all | solution.py:362
  72.6 2.0 %relay.1 = (bf16[64,1536]{1,0:T(8,128)(2,1)S(1)}, bf16[512,1152]{1,0:T(8,128)(2,1)S(1)}) custom-call(bf16[512,1152]{1,0:T(8,128)(2,1)S(1)} %bitcast.27, bf16[3,128,512]{2,1,0:T(8,128)(2,1)} %copy-done.5, bf16[3,512,256]{2,1,0:T(8,128)(2,1)} %copy-done.3, bf16[2,64,1536]{2,1,0:T(8,128)(2,1)} %grads_ref.3), custom_call_target="tpu_custom_call" | custom-call | flops 500000000 | bytes 4000000 | tf_op jit(solution)/shard_map/relay/pallas_call | solution.py:319
  74.6 0.0 copy-start
  74.6 0.7 copy-done
  75.3 23.0 %all_to_all.21 = bf16[64,8,1152]{2,1,0:T(8,128)(2,1)S(1)} all-to-all(bf16[64,8,1152]{2,1,0:T(8,128)(2,1)S(1)} %bitcast.28), channel_id=1, replica_groups=mesh['section'=2,'ep'=64] {'ep'}, dimensions={0} | all-to-all | bytes 2359296 | tf_op jit(solution)/shard_map/all_to_all | solution.py:362
  98.2 10.6 %expert_layer_0.1 = bf16[512,1152]{1,0:T(8,128)(2,1)} custom-call(bf16[512,1152]{1,0:T(8,128)(2,1)S(1)} %bitcast.24, bf16[2,384,3072]{2,1,0:T(8,128)(2,1)} %bitcast.37, bf16[384,3072]{1,0:T(8,128)(2,1)S(1)} %collective-permute-done.2.refs_2_, bf16[1536,1536]{1,0:T(8,128)(2,1)} %bitcast.43, bf16[1536,1536]{1,0:T(8,128)(2,1)} %copy-done.8, ...), custom_call_target="tpu_custom_call" | custom-call | flops 5435817984 | bytes 20000000 | tf_op jit(solution)/shard_map/expert_layer_0/pallas_call | solution.py:427
  108.9 5.8 %all-to-all-start.3 = ((bf16[64,8,1152]{2,1,0:T(8,128)(2,1)}), bf16[64,8,1152]{2,1,0:T(8,128)(2,1)S(1)}, u32[]{:S(2)}, u32[]{:S(2)}) async-start(bf16[64,8,1152]{2,1,0:T(8,128)(2,1)} %bitcast.15), calls=%async_computation.3 | async-start | bytes 2359296 | tf_op jit(solution)/shard_map/all_to_all | solution.py:362
  114.7 0.0 copy-start.1
  114.8 17.4 %all-to-all-done.3 = bf16[64,8,1152]{2,1,0:T(8,128)(2,1)S(1)} async-done(((bf16[64,8,1152]{2,1,0:T(8,128)(2,1)}), bf16[64,8,1152]{2,1,0:T(8,128)(2,1)S(1)}, u32[]{:S(2)}, u32[]{:S(2)}) %all-to-all-start.3) | async-done | bytes 1179680 | tf_op jit(solution)/shard_map/all_to_all | solution.py:362
  132.2 1.4 %gather_last.1 = bf16[64,1536]{1,0:T(8,128)(2,1)S(1)} custom-call(bf16[512,1152]{1,0:T(8,128)(2,1)S(1)} %bitcast.26, bf16[3,128,512]{2,1,0:T(8,128)(2,1)} %copy-done.4, bf16[64,1536]{1,0:T(8,128)(2,1)} %copy-done), custom_call_target="tpu_custom_call" | custom-call | flops 200000000 | bytes 4000000 | tf_op jit(solution)/shard_map/gather_last/pallas_call | solution.py:319
  133.6 0.0 copy-done.1
  133.7 3.6 %collective-permute-start.5 = (bf16[64,1536]{1,0:T(8,128)(2,1)S(1)}, bf16[64,1536]{1,0:T(8,128)(2,1)S(1)}, u32[]{:S(2)}, u32[]{:S(2)}) collective-permute-start(bf16[64,1536]{1,0:T(8,128)(2,1)S(1)} %broadcast_select_fusion), channel_id=1, source_target_pairs={{0,64},{64,0},{1,65},{65,1},{2,66},{66,2},{3,67},{67,3},{4,68},{68... | collective-permute-start | bytes 589832 | tf_op jit(solution)/shard_map/ppermute | solution.py:368
  137.3 1.1 collective-permute-done.5
  138.4 0.8 maximum_bitcast_fusion
  (2 shorter events, 0.1 us)
Async XLA Ops:
  0.0 2.5 %collective-permute-start = (s32[2,4,64]{2,1,0:T(4,128)}, s32[2,4,64]{2,1,0:T(4,128)S(1)}, u32[]{:S(2)}, u32[]{:S(2)}) collective-permute-start(s32[2,4,64]{2,1,0:T(4,128)} %bitcast.29), channel_id=1, source_target_pairs={{0,64},{64,0},{1,65},{65,1},{2,66},{66,2},{3,67},{67,3},{4,68},{68... | collective-permute-start | bytes 6152 | tf_op jit(solution)/shard_map/ppermute | solution.py:368
  1.4 1.4 collective-permute-start.1
  2.8 33.9 %collective-permute-start.4 = (bf16[1536,3072]{1,0:T(8,128)(2,1)}, bf16[1536,3072]{1,0:T(8,128)(2,1)}, u32[]{:S(2)}, u32[]{:S(2)}) collective-permute-start(bf16[1536,3072]{1,0:T(8,128)(2,1)} %bitcast.38), channel_id=1, source_target_pairs={{0,64},{64,0},{1,65},{65,1},{2,66},{66,2},{3,67},{67,3},{4,68},{68... | collective-permute-start | bytes 28311560 | tf_op jit(solution)/shard_map/ppermute | solution.py:368
  3.0 33.8 %collective-permute-start.3 = (bf16[1536,1536]{1,0:T(8,128)(2,1)}, bf16[1536,1536]{1,0:T(8,128)(2,1)S(1)}, u32[]{:S(2)}, u32[]{:S(2)}) collective-permute-start(bf16[1536,1536]{1,0:T(8,128)(2,1)} %bitcast.41), channel_id=1, source_target_pairs={{0,64},{64,0},{1,65},{65,1},{2,66},{66,2},{3,67},{67,3},{4,68},{68... | collective-permute-start | bytes 14155784 | tf_op jit(solution)/shard_map/ppermute | solution.py:368
  3.3 2.1 %copy-start.2 = (bf16[2,64,1536]{2,1,0:T(8,128)(2,1)S(1)}, bf16[2,64,1536]{2,1,0:T(8,128)(2,1)}, u32[]{:S(2)}) copy-start(bf16[2,64,1536]{2,1,0:T(8,128)(2,1)} %grads_ref.3) | copy-start | bytes 1179652
  3.3 2.1 %copy-start.6 = (s32[1,2,64,4]{2,3,1,0:T(4,128)S(1)}, s32[1,2,64,4]{2,3,1,0:T(4,128)}, u32[]{:S(2)}) copy-start(s32[1,2,64,4]{2,3,1,0:T(4,128)} %param.7) | copy-start | bytes 6148
  3.3 2.1 %copy-start.7 = (f32[1,2,64,4]{2,3,1,0:T(4,128)S(1)}, f32[1,2,64,4]{2,3,1,0:T(4,128)}, u32[]{:S(2)}) copy-start(f32[1,2,64,4]{2,3,1,0:T(4,128)} %param.8) | copy-start | bytes 6148
  5.2 31.6 %collective-permute-start.2 = (bf16[384,3072]{1,0:T(8,128)(2,1)S(1)}, bf16[384,3072]{1,0:T(8,128)(2,1)S(1)}, u32[]{:S(2)}, u32[]{:S(2)}) collective-permute-start(bf16[384,3072]{1,0:T(8,128)(2,1)S(1)} %other_pre.1), channel_id=1, source_target_pairs={{0,64},{64,0},{1,65},{65,1},{2,66},{66,2},{3,67},{67,3},{4,68},{68... | collective-permute-start | bytes 7077896 | tf_op jit(solution)/shard_map/ppermute | solution.py:368
  36.7 2.2 %copy-start.8 = (bf16[1536,1536]{1,0:T(8,128)(2,1)}, bf16[1536,1536]{1,0:T(8,128)(2,1)S(1)}, u32[]{:S(2)}) copy-start(bf16[1536,1536]{1,0:T(8,128)(2,1)S(1)} %collective-permute-done.3.refs_4_) | copy-start | bytes 14155780
  49.8 22.8 %all-to-all-start.1 = ((bf16[64,8,1152]{2,1,0:T(8,128)(2,1)}), bf16[64,8,1152]{2,1,0:T(8,128)(2,1)S(1)}, u32[]{:S(2)}, u32[]{:S(2)}) async-start(bf16[64,8,1152]{2,1,0:T(8,128)(2,1)} %bitcast.11), calls=%async_computation.1 | async-start | bytes 2359296 | tf_op jit(solution)/shard_map/all_to_all | solution.py:362
  56.4 0.9 copy-start.3
  57.3 0.8 copy-start.4
  58.1 0.7 copy-start.5
  74.6 0.7 copy-start
  108.9 23.3 %all-to-all-start.3 = ((bf16[64,8,1152]{2,1,0:T(8,128)(2,1)}), bf16[64,8,1152]{2,1,0:T(8,128)(2,1)S(1)}, u32[]{:S(2)}, u32[]{:S(2)}) async-start(bf16[64,8,1152]{2,1,0:T(8,128)(2,1)} %bitcast.15), calls=%async_computation.3 | async-start | bytes 2359296 | tf_op jit(solution)/shard_map/all_to_all | solution.py:362
  114.7 18.9 %copy-start.1 = (bf16[64,1536]{1,0:T(8,128)(2,1)S(1)}, bf16[64,1536]{1,0:T(8,128)(2,1)}, u32[]{:S(2)}) copy-start(bf16[64,1536]{1,0:T(8,128)(2,1)} %copy-done) | copy-start | bytes 589828
  133.7 4.7 %collective-permute-start.5 = (bf16[64,1536]{1,0:T(8,128)(2,1)S(1)}, bf16[64,1536]{1,0:T(8,128)(2,1)S(1)}, u32[]{:S(2)}, u32[]{:S(2)}) collective-permute-start(bf16[64,1536]{1,0:T(8,128)(2,1)S(1)} %broadcast_select_fusion), channel_id=1, source_target_pairs={{0,64},{64,0},{1,65},{65,1},{2,66},{66,2},{3,67},{67,3},{4,68},{68... | collective-permute-start | bytes 589832 | tf_op jit(solution)/shard_map/ppermute | solution.py:368

commit v3 on v2

--- a/solution.py
+++ b/solution.py
@@ -148,37 +148,94 @@
     send_rows(masks, grads[...], out_ref)
 
 
-def routes_kernel(
-    own_ids, own_w, got_ids, got_w, send_ref, gather_one_ref, gather_zero_ref,
-    ids_one, ids_zero, weights, sem,
-):
-    fetch((own_ids,), (got_ids,), 1, ((ids_one, 0),), sem)
-    fetch((own_ids, own_w), (got_ids, got_w), 0, ((ids_zero, 1), (weights, 2)), sem)
-    settle(own_ids.at[0], ids_one, sem.at[0])
-    settle(own_ids.at[0], ids_zero, sem.at[1])
-    settle(own_w.at[0], weights, sem.at[2])
-    for ids, out in ((ids_one, gather_one_ref), (ids_zero, gather_zero_ref)):
-        for part, mask in enumerate(gather_masks(lanes(ids[...].astype(F32), 2))):
-            out[part] = mask.T.astype(BF)
-    masks = send_masks(lanes(ids_zero[...].astype(F32), 4), lanes(weights[...], 4))
-    for part, mask in enumerate(masks):
-        send_ref[part] = mask
-
-
-def other_kernel(pre_ref, out_ref, held, sems):
+def other_kernel(pre_ref, out_ref, sems):
     section = lax.axis_index("section")
-    into, out = [], []
+    copies = []
     for piece in range(PIECES):
         here = pl.ds(piece * (SLOTS // PIECES), SLOTS // PIECES)
-        into.append(pltpu.make_async_copy(pre_ref.at[1 - section, here], held.at[here], sems.at[0, piece]))
-        out.append(pltpu.make_async_copy(held.at[here], out_ref.at[here], sems.at[1, piece]))
-    for copy in into:
+        copies.append(
+            pltpu.make_async_copy(pre_ref.at[1 - section, here], out_ref.at[here], sems.at[piece])
+        )
+    for copy in copies:
         copy.start()
-    for piece in range(PIECES):
-        into[piece].wait()
-        out[piece].start()
-    for copy in out:
+    for copy in copies:
         copy.wait()
+
+
+def factors(gate, linear):
+    sigmoid = jax.nn.sigmoid(alpha_glu * gate)
+    for_gate = (linear + 1.0) * sigmoid * (1.0 + alpha_glu * gate * (1.0 - sigmoid))
+    return for_gate, gate * sigmoid
+
+
+def factors_kernel(pre_ref, first_ref, second_ref, held, made, sems):
+    working = lax.axis_index("section") == 0
+    size = SLOTS // PIECES
+    pieces = [(micro, piece) for micro in (0, 1) for piece in range(PIECES)]
+
+    def into(micro, piece):
+        here = pl.ds(piece * size, size)
+        return pltpu.make_async_copy(
+            pre_ref.at[micro, here], held.at[micro, here], sems.at[0, micro, piece]
+        )
+
+    def out(micro, piece):
+        here = pl.ds(piece * size, size)
+        target = (first_ref, second_ref)[micro]
+        return pltpu.make_async_copy(made.at[micro, here], target.at[here], sems.at[1, micro, piece])
+
+    @pl.when(working)
+    def _():
+        for micro, piece in pieces:
+            into(micro, piece).start()
+
+    @pl.when(working)
+    def _():
+        for micro, piece in pieces:
+            into(micro, piece).wait()
+            here = slice(piece * size, (piece + 1) * size)
+            for_gate, for_up = factors(
+                held[micro, here, :HIDDEN].astype(F32), held[micro, here, HIDDEN:].astype(F32)
+            )
+            made[micro, here, :HIDDEN] = for_gate.astype(BF)
+            made[micro, here, HIDDEN:] = for_up.astype(BF)
+            out(micro, piece).start()
+        for micro, piece in pieces:
+            out(micro, piece).wait()
+
+
+def routes_kernel(mine, own_ids, own_w, got_ids, got_w, *refs):
+    outs = refs[-10:-7]
+    ids_one, ids_zero, weights, send, gather_one, gather_zero, sem = refs[-7:]
+    working = lax.axis_index("section") == mine
+    one = got_ids if mine == 0 else own_ids
+    ids, w = (own_ids, own_w) if mine == 0 else (got_ids, got_w)
+    picks = [
+        pltpu.make_async_copy(one.at[mine], ids_one, sem.at[0]),
+        pltpu.make_async_copy(ids.at[mine], ids_zero, sem.at[1]),
+        pltpu.make_async_copy(w.at[mine], weights, sem.at[2]),
+    ]
+    masks_out = [
+        pltpu.make_async_copy(value, target, sem.at[3 + place])
+        for place, (value, target) in enumerate(zip((send, gather_one, gather_zero), outs))
+    ]
+
+    @pl.when(working)
+    def _():
+        for copy in picks:
+            copy.start()
+        for copy in picks:
+            copy.wait()
+        for ids_held, target in ((ids_one, gather_one), (ids_zero, gather_zero)):
+            for part, mask in enumerate(gather_masks(lanes(ids_held[...].astype(F32), 2))):
+                target[part] = mask.T.astype(BF)
+        masks = send_masks(lanes(ids_zero[...].astype(F32), 4), lanes(weights[...], 4))
+        for part, mask in enumerate(masks):
+            send[part] = mask
+        for copy in masks_out:
+            copy.start()
+        for copy in masks_out:
+            copy.wait()
 
 
 def relay_kernel(
@@ -245,7 +302,7 @@
     @pl.when(section == layer)
     def _():
         for step in range(2 * STEPS):
-            for copy in copies(step, own_pre.at[layer], own_down, own_up):
+            for copy in copies(step, own_pre.at[1] if layer else own_pre, own_down, own_up):
                 copy.start()
 
     @pl.when(section != layer)
@@ -279,13 +336,11 @@
         for ready in range(step, step + FIRST_WAITS):
             finish(ready)
         back = dot(rows[...], down[here, :], ((1,), (1,)))
-        gate = pre[:, here].astype(F32)
-        linear = pre[:, there].astype(F32)
-        sigmoid = jax.nn.sigmoid(alpha_glu * gate)
-        joined[:, there] = (back * gate * sigmoid).astype(BF)
-        joined[:, here] = (
-            back * (linear + 1.0) * sigmoid * (1.0 + alpha_glu * gate * (1.0 - sigmoid))
-        ).astype(BF)
+        for_gate, for_up = pre[:, here].astype(F32), pre[:, there].astype(F32)
+        if layer == 1:
+            for_gate, for_up = factors(for_gate, for_up)
+        joined[:, here] = (back * for_gate).astype(BF)
+        joined[:, there] = (back * for_up).astype(BF)
     for step in range(0, STEPS, SECOND_WAITS):
         here = slice(step * TILE, (step + SECOND_WAITS) * TILE)
         for ready in range(step, step + SECOND_WAITS):
@@ -307,6 +362,8 @@
 
 NEAR = pl.BlockSpec(memory_space=pltpu.VMEM)
 FAR = pl.BlockSpec(memory_space=pl.ANY)
+PICK_IDS = pltpu.VMEM((TOP, TOKENS), jnp.int32)
+PICK_WEIGHTS = pltpu.VMEM((TOP, TOKENS), F32)
 MASKS = [(3, ROWS, 4 * TOKENS), (3, 2 * TOKENS, ROWS), (3, 2 * TOKENS, ROWS)]
 
 
@@ -321,18 +378,49 @@
     return run
 
 
-def small_call(kernel, outs, ins, scratch, copies, name, flops, out_specs=NEAR, still=False):
+def small_call(
+    kernel, outs, ins, scratch, copies, name, flops, out_specs=NEAR, still=False, limit=BIG, aliases={},
+    cost=4_000_000,
+):
     call = pl.pallas_call(
         kernel,
         out_shape=outs,
         in_specs=ins,
         out_specs=out_specs,
         name=name,
+        input_output_aliases=aliases,
         scratch_shapes=scratch + [pltpu.SemaphoreType.DMA(copies)],
-        compiler_params=pltpu.CompilerParams(vmem_limit_bytes=BIG),
-        cost_estimate=pl.CostEstimate(flops=flops, bytes_accessed=4_000_000, transcendentals=0),
+        compiler_params=pltpu.CompilerParams(vmem_limit_bytes=limit),
+        cost_estimate=pl.CostEstimate(flops=flops, bytes_accessed=cost, transcendentals=0),
     )
     return call_far(ins, call) if still else call
+
+
+def factors_call(pre):
+    return small_call(
+        factors_kernel,
+        [pltpu.HBM((SLOTS, 2 * HIDDEN), BF)] * 2,
+        [FAR],
+        [pltpu.VMEM((2, SLOTS, 2 * HIDDEN), BF)] * 2,
+        (2, 2, PIECES),
+        "lower_factors",
+        20_000_000,
+        [FAR] * 2,
+    )(pre)
+
+
+def routes_call(mine, *operands):
+    return small_call(
+        lambda *refs: routes_kernel(mine, *refs),
+        [pltpu.HBM(dims, BF) for dims in MASKS],
+        [FAR] * len(operands),
+        [PICK_IDS, PICK_IDS, PICK_WEIGHTS] + [pltpu.VMEM(dims, BF) for dims in MASKS],
+        (6,),
+        f"routes_section_{mine}",
+        1_000_000_000,
+        [FAR] * 3,
+        aliases={4 + place: place for place in range(len(operands) - 4)},
+    )(*operands)
 
 
 def expert_call(layer):
@@ -372,6 +460,10 @@
     return lax.optimization_barrier((value,) + others)[0]
 
 
+def after_all(values, *others):
+    return lax.optimization_barrier(tuple(values) + others)[: len(values)]
+
+
 def body(top_grads, expert_ids, route_weights, preacts, w_gate_up, w_down):
     section = lax.axis_index("section")
     own_ids = expert_ids[0].transpose(0, 2, 1)
@@ -380,37 +472,31 @@
     own_down, own_up = w_down[0, 0], w_gate_up[0, 0]
     got_ids, got_w = swapped(own_ids), swapped(own_w)
     other_pre = small_call(
-        other_kernel,
-        shape(SLOTS, 2 * HIDDEN),
-        [FAR],
-        [pltpu.VMEM((SLOTS, 2 * HIDDEN), BF)],
-        (2, PIECES),
-        "other_pre",
-        1_000_000,
-        FAR,
+        other_kernel, shape(SLOTS, 2 * HIDDEN), [FAR], [], (PIECES,), "other_pre", 1_000_000
     )(own_pre)
     got_down = swapped(after(own_down, got_ids, got_w))
     got_up = swapped(after(own_up, got_ids, got_w))
     got_pre = swapped(other_pre)
-
-    picks = [pltpu.VMEM((TOP, TOKENS), jnp.int32), pltpu.VMEM((TOP, TOKENS), F32)]
+    picks = (own_ids, own_w, got_ids, got_w)
+
+    own_factors, other_factors = factors_call(after(own_pre, got_ids, got_w, other_pre))
+    masks = routes_call(0, own_ids, own_w, after(got_ids, own_factors), got_w)
+
     grads = pltpu.VMEM((TOKENS, MODEL), BF)
     packed = small_call(
-        first_kernel, shape(ROWS, WIDE), [FAR] * 5, picks + [grads], (3,), "send_first", 300_000_000
-    )(own_ids, own_w, got_ids, got_w, top_grads)
-    send_zero, gather_one, gather_zero = small_call(
-        routes_kernel,
-        [shape(*dims) for dims in MASKS],
-        [FAR] * 4,
-        picks[:1] + picks,
+        first_kernel,
+        shape(ROWS, WIDE),
+        [FAR] * 5,
+        [PICK_IDS, PICK_WEIGHTS, grads],
         (3,),
-        "routes",
-        1_000_000_000,
-        [NEAR] * 3,
-    )(own_ids, own_w, after(got_ids, packed), got_w)
+        "send_first",
+        300_000_000,
+    )(own_ids, own_w, after(got_ids, *masks), got_w, top_grads)
     arrived = exchange(packed)
-    operands = (own_pre, got_pre, own_down, got_down, own_up, got_up)
-    answered = expert_call(1)(arrived, *operands)
+    weights = (own_down, got_down, own_up, got_up)
+    answered = expert_call(1)(arrived, own_pre, got_pre, *weights)
+    got_factors = lax.ppermute(after(other_factors, answered), "section", [(0, 1)])
+    send_zero, gather_one, gather_zero = routes_call(1, *picks, *after_all(masks, answered))
     returned = exchange(answered)
     lower, packed = small_call(
         relay_kernel,
@@ -424,7 +510,7 @@
         True,
     )(returned, gather_one, send_zero, top_grads)
     arrived = exchange(packed)
-    answered = expert_call(0)(arrived, *operands)
+    answered = expert_call(0)(arrived, own_factors, got_factors, *weights)
     returned = exchange(answered)
     final = small_call(
         last_kernel,

time: 140 us -> 128 us (0.914)
  blocking collectives: 52.8 us -> 43.8 us
  waiting for transfers between devices: 33.6 us -> 26.9 us
  starting transfers between devices: 16.6 us -> 23 us
  local copies, waits for them, and re-layouts: 5.32 us -> 1.91 us
    all_to_all x2, blocking collectives: 52.8 us -> 43.8 us  [exchange(): lax.all_to_all(packed.reshape(EXPERTS, PACK, WIDE), 'ep', split_axis=0, c...]
    all_to_all x2, waiting for transfers between devices: 31.2 us -> 24.4 us  [exchange(): lax.all_to_all(packed.reshape(EXPERTS, PACK, WIDE), 'ep', split_axis=0, c...]
    ppermute x6, starting transfers between devices: 5.82 us -> 11.9 us  [swapped(): return lax.ppermute(value, 'section', [(0, 1), (1, 0)])]
    unnamed x18 -> x16, local copies, waits for them, and re-layouts: 5.32 us -> 1.91 us
    pallas_call x5 -> x7, Pallas kernels: 26.4 us -> 27.5 us  [the longest x1 10.8 us: body(): answered = expert_call(1)(arrived, own_pre, got_pre, *weights)]
  transfers between devices with their start and end apart: 8 -> 9, of which waited for: 5 -> 5; matrix products, arithmetic and copies ran while one was open for 0% -> 0% of each run, Pallas kernels for 4% -> 6%
where the time goes in v3:
time: 128 us
  blocking collectives  43.8 us (34%)
  Pallas kernels  31.1 us (24%)
  waiting for transfers between devices  26.9 us (21%)
  starting transfers between devices  23 us (18%)
  local copies, waits for them, and re-layouts  1.91 us (1%)
    all_to_all x2, blocking collectives, exchange(): lax.all_to_all(packed.reshape(EXPERTS, PACK, WIDE), 'ep', split_axis=0, c...  43.8 us
    all_to_all x2, waiting for transfers between devices, exchange(): lax.all_to_all(packed.reshape(EXPERTS, PACK, WIDE), 'ep', split_axis=0, c...  24.4 us
    ppermute x6, starting transfers between devices, swapped(): return lax.ppermute(value, 'section', [(0, 1), (1, 0)])  11.9 us
    pallas_call x1, Pallas kernels, body(): answered = expert_call(1)(arrived, own_pre, got_pre, *weights)  10.8 us
    pallas_call x1, Pallas kernels, body(): answered = expert_call(0)(arrived, own_factors, got_factors, *weights)  10.7 us
    all_to_all x2, starting transfers between devices, exchange(): lax.all_to_all(packed.reshape(EXPERTS, PACK, WIDE), 'ep', split_axis=0, c...  9.81 us
    pallas_call x2, Pallas kernels, run(): return call(*kept)  3.61 us
    pallas_call x2, Pallas kernels, routes_call(): small_call(lambda *refs: routes_kernel(mine, *refs), [pltpu.HBM(dims, BF)...  2.72 us
  transfers between devices with their start and end apart: 9, of which 5 were waited for; matrix products, arithmetic and copies ran while one was open for 0% of the time, Pallas kernels for 6%

profile of v3, /device:TPU:1, one launch (start us, length us, event | category | flops | bytes accessed | tf_op | source)
XLA Modules:
  0.0 127.7 jit_solution(16910845619110902491)
XLA Ops:
  0.0 1.4 %collective-permute-start = (s32[2,4,64]{2,1,0:T(4,128)}, s32[2,4,64]{2,1,0:T(4,128)S(1)}, u32[]{:S(2)}, u32[]{:S(2)}) collective-permute-start(s32[2,4,64]{2,1,0:T(4,128)} %bitcast.32), channel_id=1, source_target_pairs={{0,64},{64,0},{1,65},{65,1},{2,66},{66,2},{3,67},{67,3},{4,68},{68... | collective-permute-start | bytes 6152 | tf_op jit(solution)/shard_map/ppermute | solution.py:456
  1.4 0.0 collective-permute-start.1
  1.4 1.0 collective-permute-done.refs_2_.got_ids
  2.5 0.3 collective-permute-done.1.refs_3_.got_w
  2.8 0.2 collective-permute-start.4
  3.0 0.3 collective-permute-start.3
  3.3 0.0 copy-start
  3.3 1.8 %other_pre.1 = bf16[384,3072]{1,0:T(8,128)(2,1)S(1)} custom-call(bf16[2,384,3072]{2,1,0:T(8,128)(2,1)} %bitcast.23), custom_call_target="tpu_custom_call" | custom-call | flops 1000000 | bytes 4000000 | tf_op jit(solution)/shard_map/other_pre/pallas_call | solution.py:474
  5.1 0.0 copy-start.5
  5.1 0.0 copy-start.6
  5.1 0.2 collective-permute-start.2
  5.4 1.0 copy-done
  6.4 0.1 lower_factors.1
  6.5 0.0 copy-start.4
  6.5 0.0 copy-done.5
  6.5 0.0 copy-done.6
  6.5 0.1 routes_section_0.1
  6.6 0.9 copy-done.4
  7.5 1.4 %send_first.1 = bf16[512,1152]{1,0:T(8,128)(2,1)S(1)} custom-call(s32[2,4,64]{2,1,0:T(4,128)S(1)} %bitcast.34, f32[2,4,64]{2,1,0:T(4,128)S(1)} %bitcast.38, s32[2,4,64]{2,1,0:T(4,128)S(1)} %collective-permute-done.refs_2_.got_ids, f32[2,4,64]{2,1,0:T(4,128)S(1)} %collective-permute-done.1.refs_3_.got_w, bf16[2,64,1536]{2,1,0:T(8,128)(2,1)S(1)} %copy-done.4), custom_call_target="tpu_custom_call" | custom-call | flops 300000000 | bytes 4000000 | tf_op jit(solution)/shard_map/send_first/pallas_call | solution.py:486
  8.9 25.4 %all_to_all.20 = bf16[64,8,1152]{2,1,0:T(8,128)(2,1)S(1)} all-to-all(bf16[64,8,1152]{2,1,0:T(8,128)(2,1)S(1)} %bitcast.28), channel_id=1, replica_groups=mesh['section'=2,'ep'=64] {'ep'}, dimensions={0} | all-to-all | bytes 2359296 | tf_op jit(solution)/shard_map/all_to_all | solution.py:450
  34.3 0.0 collective-permute-done.2.refs_2_
  34.3 0.0 collective-permute-done.3.refs_4_
  34.3 0.0 collective-permute-done.4.refs_6_
  34.3 10.8 %expert_layer_1.1 = bf16[512,1152]{1,0:T(8,128)(2,1)} custom-call(bf16[512,1152]{1,0:T(8,128)(2,1)S(1)} %bitcast.26, bf16[2,384,3072]{2,1,0:T(8,128)(2,1)} %bitcast.24, bf16[384,3072]{1,0:T(8,128)(2,1)S(1)} %collective-permute-done.2.refs_2_, bf16[1536,1536]{1,0:T(8,128)(2,1)} %bitcast.44, bf16[1536,1536]{1,0:T(8,128)(2,1)} %collective-permute-done.3.refs_4_, ...), custom_call_target="tpu_custom_call" | custom-call | flops 5435817984 | bytes 20000000 | tf_op jit(solution)/shard_map/expert_layer_1/pallas_call | solution.py:497
  45.1 0.0 copy-start.7
  45.1 4.9 %all-to-all-start.1 = ((bf16[64,8,1152]{2,1,0:T(8,128)(2,1)}), bf16[64,8,1152]{2,1,0:T(8,128)(2,1)S(1)}, u32[]{:S(2)}, u32[]{:S(2)}) async-start(bf16[64,8,1152]{2,1,0:T(8,128)(2,1)} %bitcast.11), calls=%async_computation.1 | async-start | bytes 2359296 | tf_op jit(solution)/shard_map/all_to_all | solution.py:450
  50.1 0.0 copy-done.7
  50.1 1.3 %collective-permute-start.5 = (bf16[384,3072]{1,0:T(8,128)(2,1)S(1)}, bf16[384,3072]{1,0:T(8,128)(2,1)}, u32[]{:S(2)}, u32[]{:S(2)}) collective-permute-start(bf16[384,3072]{1,0:T(8,128)(2,1)S(1)} %copy-done.7), channel_id=1, source_target_pairs={{0,64},{1,65},{2,66},{3,67},{4,68},{5,69},{6,70},{7,71},{8,72},{9,... | collective-permute-start | bytes 7077896 | tf_op jit(solution)/shard_map/ppermute | solution.py:498
  51.4 2.7 %routes_section_1.1 = (bf16[3,512,256]{2,1,0:T(8,128)(2,1)}, bf16[3,128,512]{2,1,0:T(8,128)(2,1)}, bf16[3,128,512]{2,1,0:T(8,128)(2,1)}) custom-call(s32[2,4,64]{2,1,0:T(4,128)S(1)} %bitcast.35, f32[2,4,64]{2,1,0:T(4,128)S(1)} %bitcast.39, ...), custom_call_target="tpu_custom_call", output_to_operand_aliasing={{0}: (4, {}), {1}: (5, {}), {2}: (6, {})} | custom-call | flops 1000000000 | bytes 4000000 | tf_op jit(solution)/shard_map/routes_section_1/pallas_call | solution.py:413
  54.1 10.2 %all-to-all-done.1 = bf16[64,8,1152]{2,1,0:T(8,128)(2,1)S(1)} async-done(((bf16[64,8,1152]{2,1,0:T(8,128)(2,1)}), bf16[64,8,1152]{2,1,0:T(8,128)(2,1)S(1)}, u32[]{:S(2)}, u32[]{:S(2)}) %all-to-all-start.1) | async-done | bytes 1179680 | tf_op jit(solution)/shard_map/all_to_all | solution.py:450
  64.3 0.0 copy-start.1
  64.3 2.2 %relay.1 = (bf16[64,1536]{1,0:T(8,128)(2,1)S(1)}, bf16[512,1152]{1,0:T(8,128)(2,1)S(1)}) custom-call(bf16[512,1152]{1,0:T(8,128)(2,1)S(1)} %bitcast.30, bf16[3,128,512]{2,1,0:T(8,128)(2,1)} %get-tuple-element.36.gather_ref, bf16[3,512,256]{2,1,0:T(8,128)(2,1)} %get-tuple-element.37.send_ref, bf16[2,64,1536]{2,1,0:T(8,128)(2,1)} %grads_ref.3), custom_call_target="tpu_custom_call" | custom-call | flops 500000000 | bytes 4000000 | tf_op jit(solution)/shard_map/relay/pallas_call | solution.py:376
  66.5 0.0 copy-start.2
  66.5 18.4 %all_to_all.21 = bf16[64,8,1152]{2,1,0:T(8,128)(2,1)S(1)} all-to-all(bf16[64,8,1152]{2,1,0:T(8,128)(2,1)S(1)} %bitcast.31), channel_id=1, replica_groups=mesh['section'=2,'ep'=64] {'ep'}, dimensions={0} | all-to-all | bytes 2359296 | tf_op jit(solution)/shard_map/all_to_all | solution.py:450
  84.9 0.0 collective-permute-done.5.refs_2_
  84.9 0.0 copy-done.1
  84.9 10.7 %expert_layer_0.1 = bf16[512,1152]{1,0:T(8,128)(2,1)} custom-call(bf16[512,1152]{1,0:T(8,128)(2,1)S(1)} %bitcast.27, bf16[384,3072]{1,0:T(8,128)(2,1)S(1)} %copy-done.1, bf16[384,3072]{1,0:T(8,128)(2,1)} %collective-permute-done.5.refs_2_, bf16[1536,1536]{1,0:T(8,128)(2,1)} %bitcast.45, bf16[1536,1536]{1,0:T(8,128)(2,1)} %collective-permute-done.3.refs_4_, ...), custom_call_target="tpu_custom_call" | custom-call | flops 5435817984 | bytes 20000000 | tf_op jit(solution)/shard_map/expert_layer_0/pallas_call | solution.py:513
  95.6 0.0 copy-done.2
  95.6 0.0 copy-start.3
  95.6 4.9 %all-to-all-start.3 = ((bf16[64,8,1152]{2,1,0:T(8,128)(2,1)}), bf16[64,8,1152]{2,1,0:T(8,128)(2,1)S(1)}, u32[]{:S(2)}, u32[]{:S(2)}) async-start(bf16[64,8,1152]{2,1,0:T(8,128)(2,1)} %bitcast.15), calls=%async_computation.3 | async-start | bytes 2359296 | tf_op jit(solution)/shard_map/all_to_all | solution.py:450
  100.5 14.2 %all-to-all-done.3 = bf16[64,8,1152]{2,1,0:T(8,128)(2,1)S(1)} async-done(((bf16[64,8,1152]{2,1,0:T(8,128)(2,1)}), bf16[64,8,1152]{2,1,0:T(8,128)(2,1)S(1)}, u32[]{:S(2)}, u32[]{:S(2)}) %all-to-all-start.3) | async-done | bytes 1179680 | tf_op jit(solution)/shard_map/all_to_all | solution.py:450
  114.6 1.4 %gather_last.1 = bf16[64,1536]{1,0:T(8,128)(2,1)S(1)} custom-call(bf16[512,1152]{1,0:T(8,128)(2,1)S(1)} %bitcast.29, bf16[3,128,512]{2,1,0:T(8,128)(2,1)} %get-tuple-element.41.gather_ref, bf16[64,1536]{1,0:T(8,128)(2,1)} %copy-done.2), custom_call_target="tpu_custom_call" | custom-call | flops 200000000 | bytes 4000000 | tf_op jit(solution)/shard_map/gather_last/pallas_call | solution.py:376
  116.1 0.0 copy-done.3
  116.1 9.7 %collective-permute-start.6 = (bf16[64,1536]{1,0:T(8,128)(2,1)S(1)}, bf16[64,1536]{1,0:T(8,128)(2,1)S(1)}, u32[]{:S(2)}, u32[]{:S(2)}) collective-permute-start(bf16[64,1536]{1,0:T(8,128)(2,1)S(1)} %broadcast_select_fusion), channel_id=1, source_target_pairs={{0,64},{64,0},{1,65},{65,1},{2,66},{66,2},{3,67},{67,3},{4,68},{68... | collective-permute-start | bytes 589832 | tf_op jit(solution)/shard_map/ppermute | solution.py:456
  125.8 1.1 collective-permute-done.6
  126.9 0.8 maximum_bitcast_fusion
  (2 shorter events, 0.1 us)
Async XLA Ops:
  0.0 2.5 %collective-permute-start = (s32[2,4,64]{2,1,0:T(4,128)}, s32[2,4,64]{2,1,0:T(4,128)S(1)}, u32[]{:S(2)}, u32[]{:S(2)}) collective-permute-start(s32[2,4,64]{2,1,0:T(4,128)} %bitcast.32), channel_id=1, source_target_pairs={{0,64},{64,0},{1,65},{65,1},{2,66},{66,2},{3,67},{67,3},{4,68},{68... | collective-permute-start | bytes 6152 | tf_op jit(solution)/shard_map/ppermute | solution.py:456
  1.4 1.4 %collective-permute-start.1 = (f32[2,4,64]{2,1,0:T(4,128)}, f32[2,4,64]{2,1,0:T(4,128)S(1)}, u32[]{:S(2)}, u32[]{:S(2)}) collective-permute-start(f32[2,4,64]{2,1,0:T(4,128)} %bitcast.36), channel_id=1, source_target_pairs={{0,64},{64,0},{1,65},{65,1},{2,66},{66,2},{3,67},{67,3},{4,68},{68... | collective-permute-start | bytes 6152 | tf_op jit(solution)/shard_map/ppermute | solution.py:456
  2.8 31.5 %collective-permute-start.4 = (bf16[1536,3072]{1,0:T(8,128)(2,1)}, bf16[1536,3072]{1,0:T(8,128)(2,1)}, u32[]{:S(2)}, u32[]{:S(2)}) collective-permute-start(bf16[1536,3072]{1,0:T(8,128)(2,1)} %bitcast.40), channel_id=1, source_target_pairs={{0,64},{64,0},{1,65},{65,1},{2,66},{66,2},{3,67},{67,3},{4,68},{68... | collective-permute-start | bytes 28311560 | tf_op jit(solution)/shard_map/ppermute | solution.py:456
  3.0 31.4 %collective-permute-start.3 = (bf16[1536,1536]{1,0:T(8,128)(2,1)}, bf16[1536,1536]{1,0:T(8,128)(2,1)}, u32[]{:S(2)}, u32[]{:S(2)}) collective-permute-start(bf16[1536,1536]{1,0:T(8,128)(2,1)} %bitcast.43), channel_id=1, source_target_pairs={{0,64},{64,0},{1,65},{65,1},{2,66},{66,2},{3,67},{67,3},{4,68},{68... | collective-permute-start | bytes 14155784 | tf_op jit(solution)/shard_map/ppermute | solution.py:456
  3.3 3.0 %copy-start = (bf16[1,2,1,384,3072]{4,3,2,1,0:T(8,128)(2,1)S(1)}, bf16[1,2,1,384,3072]{4,3,2,1,0:T(8,128)(2,1)}, u32[]{:S(2)}) copy-start(bf16[1,2,1,384,3072]{4,3,2,1,0:T(8,128)(2,1)} %param.9) | copy-start | bytes 14155780
  5.1 1.4 %copy-start.5 = (s32[1,2,64,4]{2,3,1,0:T(4,128)S(1)}, s32[1,2,64,4]{2,3,1,0:T(4,128)}, u32[]{:S(2)}) copy-start(s32[1,2,64,4]{2,3,1,0:T(4,128)} %param.7) | copy-start | bytes 6148
  5.1 1.4 %copy-start.6 = (f32[1,2,64,4]{2,3,1,0:T(4,128)S(1)}, f32[1,2,64,4]{2,3,1,0:T(4,128)}, u32[]{:S(2)}) copy-start(f32[1,2,64,4]{2,3,1,0:T(4,128)} %param.8) | copy-start | bytes 6148
  5.1 29.2 %collective-permute-start.2 = (bf16[384,3072]{1,0:T(8,128)(2,1)S(1)}, bf16[384,3072]{1,0:T(8,128)(2,1)S(1)}, u32[]{:S(2)}, u32[]{:S(2)}) collective-permute-start(bf16[384,3072]{1,0:T(8,128)(2,1)S(1)} %other_pre.1), channel_id=1, source_target_pairs={{0,64},{64,0},{1,65},{65,1},{2,66},{66,2},{3,67},{67,3},{4,68},{68... | collective-permute-start | bytes 7077896 | tf_op jit(solution)/shard_map/ppermute | solution.py:456
  6.5 1.0 copy-start.4
  45.1 5.0 %copy-start.7 = (bf16[384,3072]{1,0:T(8,128)(2,1)S(1)}, bf16[384,3072]{1,0:T(8,128)(2,1)}, u32[]{:S(2)}) copy-start(bf16[384,3072]{1,0:T(8,128)(2,1)} %get-tuple-element.40) | copy-start | bytes 7077892
  45.1 19.2 %all-to-all-start.1 = ((bf16[64,8,1152]{2,1,0:T(8,128)(2,1)}), bf16[64,8,1152]{2,1,0:T(8,128)(2,1)S(1)}, u32[]{:S(2)}, u32[]{:S(2)}) async-start(bf16[64,8,1152]{2,1,0:T(8,128)(2,1)} %bitcast.11), calls=%async_computation.1 | async-start | bytes 2359296 | tf_op jit(solution)/shard_map/all_to_all | solution.py:450
  50.1 34.8 %collective-permute-start.5 = (bf16[384,3072]{1,0:T(8,128)(2,1)S(1)}, bf16[384,3072]{1,0:T(8,128)(2,1)}, u32[]{:S(2)}, u32[]{:S(2)}) collective-permute-start(bf16[384,3072]{1,0:T(8,128)(2,1)S(1)} %copy-done.7), channel_id=1, source_target_pairs={{0,64},{1,65},{2,66},{3,67},{4,68},{5,69},{6,70},{7,71},{8,72},{9,... | collective-permute-start | bytes 7077896 | tf_op jit(solution)/shard_map/ppermute | solution.py:498
  64.3 20.6 %copy-start.1 = (bf16[384,3072]{1,0:T(8,128)(2,1)S(1)}, bf16[384,3072]{1,0:T(8,128)(2,1)}, u32[]{:S(2)}) copy-start(bf16[384,3072]{1,0:T(8,128)(2,1)} %get-tuple-element.25.refs_1_) | copy-start | bytes 7077892
  66.5 29.1 %copy-start.2 = (bf16[64,1536]{1,0:T(8,128)(2,1)}, bf16[64,1536]{1,0:T(8,128)(2,1)S(1)}, u32[]{:S(2)}) copy-start(bf16[64,1536]{1,0:T(8,128)(2,1)S(1)} %get-tuple-element.42.grads_ref) | copy-start | bytes 589828
  95.6 20.5 %copy-start.3 = (bf16[64,1536]{1,0:T(8,128)(2,1)S(1)}, bf16[64,1536]{1,0:T(8,128)(2,1)}, u32[]{:S(2)}) copy-start(bf16[64,1536]{1,0:T(8,128)(2,1)} %copy-done.2) | copy-start | bytes 589828
  95.6 19.1 %all-to-all-start.3 = ((bf16[64,8,1152]{2,1,0:T(8,128)(2,1)}), bf16[64,8,1152]{2,1,0:T(8,128)(2,1)S(1)}, u32[]{:S(2)}, u32[]{:S(2)}) async-start(bf16[64,8,1152]{2,1,0:T(8,128)(2,1)} %bitcast.15), calls=%async_computation.3 | async-start | bytes 2359296 | tf_op jit(solution)/shard_map/all_to_all | solution.py:450
  116.1 10.8 %collective-permute-start.6 = (bf16[64,1536]{1,0:T(8,128)(2,1)S(1)}, bf16[64,1536]{1,0:T(8,128)(2,1)S(1)}, u32[]{:S(2)}, u32[]{:S(2)}) collective-permute-start(bf16[64,1536]{1,0:T(8,128)(2,1)S(1)} %broadcast_select_fusion), channel_id=1, source_target_pairs={{0,64},{64,0},{1,65},{65,1},{2,66},{66,2},{3,67},{67,3},{4,68},{68... | collective-permute-start | bytes 589832 | tf_op jit(solution)/shard_map/ppermute | solution.py:456

commit v4 on v3

--- a/solution.py
+++ b/solution.py
@@ -31,6 +31,7 @@
 PIECES = 4
 BIG = 48 * 1024 * 1024
 EXPERT_BIG = 48 * 1024 * 1024
+SMALL = 16 * 1024 * 1024
 
 
 def iota(shape, axis):
@@ -136,7 +137,7 @@
     return (grads.astype(F32) + total).astype(BF)
 
 
-def first_kernel(own_ids, own_w, got_ids, got_w, grads_ref, out_ref, ids, weights, grads, sem):
+def first_kernel(own_ids, own_w, got_ids, got_w, grads_ref, out_ref, grads, ids, weights, sem):
     section = lax.axis_index("section")
     fetch((own_ids, own_w), (got_ids, got_w), 1, ((ids, 0), (weights, 1)), sem)
     rows = pltpu.make_async_copy(grads_ref.at[section], grads, sem.at[2])
@@ -205,23 +206,17 @@
 
 
 def routes_kernel(mine, own_ids, own_w, got_ids, got_w, *refs):
-    outs = refs[-10:-7]
-    ids_one, ids_zero, weights, send, gather_one, gather_zero, sem = refs[-7:]
-    working = lax.axis_index("section") == mine
+    send, gather_one, gather_zero, ids_one, ids_zero, weights, sem = refs[-7:]
     one = got_ids if mine == 0 else own_ids
     ids, w = (own_ids, own_w) if mine == 0 else (got_ids, got_w)
-    picks = [
-        pltpu.make_async_copy(one.at[mine], ids_one, sem.at[0]),
-        pltpu.make_async_copy(ids.at[mine], ids_zero, sem.at[1]),
-        pltpu.make_async_copy(w.at[mine], weights, sem.at[2]),
-    ]
-    masks_out = [
-        pltpu.make_async_copy(value, target, sem.at[3 + place])
-        for place, (value, target) in enumerate(zip((send, gather_one, gather_zero), outs))
-    ]
-
-    @pl.when(working)
-    def _():
+
+    @pl.when(lax.axis_index("section") == mine)
+    def _():
+        picks = [
+            pltpu.make_async_copy(one.at[mine], ids_one, sem.at[0]),
+            pltpu.make_async_copy(ids.at[mine], ids_zero, sem.at[1]),
+            pltpu.make_async_copy(w.at[mine], weights, sem.at[2]),
+        ]
         for copy in picks:
             copy.start()
         for copy in picks:
@@ -232,41 +227,16 @@
         masks = send_masks(lanes(ids_zero[...].astype(F32), 4), lanes(weights[...], 4))
         for part, mask in enumerate(masks):
             send[part] = mask
-        for copy in masks_out:
-            copy.start()
-        for copy in masks_out:
-            copy.wait()
-
-
-def relay_kernel(
-    packed_ref, gather_ref, send_ref, grads_ref, lower_ref, out_ref, gather, send, grads, sem
-):
-    section = lax.axis_index("section")
-    copies = [
-        pltpu.make_async_copy(gather_ref, gather, sem.at[0]),
-        pltpu.make_async_copy(grads_ref.at[section], grads, sem.at[1]),
-        pltpu.make_async_copy(send_ref, send, sem.at[2]),
-    ]
-    for copy in copies:
-        copy.start()
-    copies[0].wait()
-    copies[1].wait()
+
+
+def relay_kernel(packed_ref, gather, send, grads, lower_ref, out_ref):
     lower = gather_rows(gather, packed_ref, grads[...])
     lower_ref[...] = lower
-    copies[2].wait()
     send_rows([send[part] for part in range(3)], lower, out_ref)
 
 
-def last_kernel(packed_ref, gather_ref, grads_ref, out_ref, gather, grads, sem):
-    copies = [
-        pltpu.make_async_copy(gather_ref, gather, sem.at[0]),
-        pltpu.make_async_copy(grads_ref, grads, sem.at[1]),
-    ]
-    for copy in copies:
-        copy.start()
-    for copy in copies:
-        copy.wait()
-    out_ref[...] = gather_rows(gather, packed_ref, grads[...])
+def last_kernel(packed_ref, gather, grads_ref, out_ref):
+    out_ref[...] = gather_rows(gather, packed_ref, grads_ref[...])
 
 
 def group_masks():
@@ -364,36 +334,37 @@
 FAR = pl.BlockSpec(memory_space=pl.ANY)
 PICK_IDS = pltpu.VMEM((TOP, TOKENS), jnp.int32)
 PICK_WEIGHTS = pltpu.VMEM((TOP, TOKENS), F32)
+KEPT = pltpu.VMEM((TOKENS, MODEL), BF)
 MASKS = [(3, ROWS, 4 * TOKENS), (3, 2 * TOKENS, ROWS), (3, 2 * TOKENS, ROWS)]
 
 
-def call_far(ins, call):
-    def run(*operands):
-        kept = [
-            pltpu.with_memory_space_constraint(value, pltpu.MemorySpace.HBM) if spec is FAR else value
-            for value, spec in zip(operands, ins)
-        ]
-        return call(*kept)
-
-    return run
+def pinned(value, space):
+    return pltpu.with_memory_space_constraint(value, space)
+
+
+def in_hbm(value):
+    return pinned(value, pltpu.MemorySpace.HBM)
+
+
+def in_vmem(value):
+    return pinned(value, pltpu.MemorySpace.VMEM)
 
 
 def small_call(
-    kernel, outs, ins, scratch, copies, name, flops, out_specs=NEAR, still=False, limit=BIG, aliases={},
-    cost=4_000_000,
+    kernel, outs, ins, scratch, copies, name, flops, out_specs=NEAR, limit=BIG, aliases={}, cost=4_000_000
 ):
-    call = pl.pallas_call(
+    sems = [pltpu.SemaphoreType.DMA(copies)] if copies else []
+    return pl.pallas_call(
         kernel,
         out_shape=outs,
         in_specs=ins,
         out_specs=out_specs,
         name=name,
         input_output_aliases=aliases,
-        scratch_shapes=scratch + [pltpu.SemaphoreType.DMA(copies)],
+        scratch_shapes=scratch + sems,
         compiler_params=pltpu.CompilerParams(vmem_limit_bytes=limit),
         cost_estimate=pl.CostEstimate(flops=flops, bytes_accessed=cost, transcendentals=0),
     )
-    return call_far(ins, call) if still else call
 
 
 def factors_call(pre):
@@ -409,21 +380,22 @@
     )(pre)
 
 
-def routes_call(mine, *operands):
+def routes_call(mine, picks, masks):
     return small_call(
         lambda *refs: routes_kernel(mine, *refs),
-        [pltpu.HBM(dims, BF) for dims in MASKS],
-        [FAR] * len(operands),
-        [PICK_IDS, PICK_IDS, PICK_WEIGHTS] + [pltpu.VMEM(dims, BF) for dims in MASKS],
-        (6,),
+        [pltpu.VMEM(dims, BF) for dims in MASKS],
+        [FAR] * 4 + [NEAR] * len(masks),
+        [PICK_IDS, PICK_IDS, PICK_WEIGHTS],
+        (3,),
         f"routes_section_{mine}",
         1_000_000_000,
-        [FAR] * 3,
-        aliases={4 + place: place for place in range(len(operands) - 4)},
-    )(*operands)
-
-
-def expert_call(layer):
+        [NEAR] * 3,
+        limit=SMALL,
+        aliases={4 + place: place for place in range(len(masks))},
+    )(*picks, *[in_vmem(mask) for mask in masks])
+
+
+def expert_call(layer, *operands):
     return pl.pallas_call(
         lambda *refs: expert_kernel(layer, *refs),
         out_shape=shape(ROWS, WIDE),
@@ -443,7 +415,7 @@
         cost_estimate=pl.CostEstimate(
             flops=6 * SLOTS * MODEL * HIDDEN, bytes_accessed=20_000_000, transcendentals=0
         ),
-    )
+    )(*operands)
 
 
 def exchange(packed):
@@ -480,49 +452,49 @@
     picks = (own_ids, own_w, got_ids, got_w)
 
     own_factors, other_factors = factors_call(after(own_pre, got_ids, got_w, other_pre))
-    masks = routes_call(0, own_ids, own_w, after(got_ids, own_factors), got_w)
-
-    grads = pltpu.VMEM((TOKENS, MODEL), BF)
-    packed = small_call(
+    masks = routes_call(0, (own_ids, own_w, after(got_ids, own_factors), got_w), ())
+
+    packed, grads = small_call(
         first_kernel,
-        shape(ROWS, WIDE),
+        [shape(ROWS, WIDE), KEPT],
         [FAR] * 5,
-        [PICK_IDS, PICK_WEIGHTS, grads],
+        [PICK_IDS, PICK_WEIGHTS],
         (3,),
         "send_first",
         300_000_000,
-    )(own_ids, own_w, after(got_ids, *masks), got_w, top_grads)
+        [NEAR] * 2,
+        limit=SMALL,
+    )(own_ids, own_w, after(got_ids, *masks), got_w, in_hbm(top_grads))
+    weights = (own_down, got_down, own_up, got_up)
     arrived = exchange(packed)
-    weights = (own_down, got_down, own_up, got_up)
-    answered = expert_call(1)(arrived, own_pre, got_pre, *weights)
+    answered = expert_call(1, arrived, own_pre, got_pre, *weights)
     got_factors = lax.ppermute(after(other_factors, answered), "section", [(0, 1)])
-    send_zero, gather_one, gather_zero = routes_call(1, *picks, *after_all(masks, answered))
+    send_zero, gather_one, gather_zero = routes_call(1, picks, after_all(masks, answered))
     returned = exchange(answered)
     lower, packed = small_call(
         relay_kernel,
-        [shape(TOKENS, MODEL), shape(ROWS, WIDE)],
-        [NEAR] + [FAR] * 3,
-        [pltpu.VMEM(MASKS[1], BF), pltpu.VMEM(MASKS[0], BF), grads],
-        (3,),
+        [KEPT, shape(ROWS, WIDE)],
+        [NEAR] * 4,
+        [],
+        (),
         "relay",
         500_000_000,
         [NEAR] * 2,
-        True,
-    )(returned, gather_one, send_zero, top_grads)
+        limit=SMALL,
+    )(returned, in_vmem(gather_one), in_vmem(send_zero), in_vmem(grads))
     arrived = exchange(packed)
-    answered = expert_call(0)(arrived, own_factors, got_factors, *weights)
+    answered = expert_call(0, arrived, own_factors, got_factors, *weights)
     returned = exchange(answered)
     final = small_call(
         last_kernel,
         shape(TOKENS, MODEL),
-        [NEAR] + [FAR] * 2,
-        [pltpu.VMEM(MASKS[2], BF), grads],
-        (2,),
+        [NEAR] * 3,
+        [],
+        (),
         "gather_last",
         200_000_000,
-        NEAR,
-        True,
-    )(returned, gather_zero, lower)
+        limit=SMALL,
+    )(returned, in_vmem(gather_zero), in_vmem(lower))
     other = swapped(jnp.where(section == 0, lower, final))
     first = jnp.where(section == 0, final, other)
     second = jnp.where(section == 0, other, lower)

time: 128 us -> 124 us (0.969)
  Pallas kernels: 31.1 us -> 27.7 us
  waiting for transfers between devices: 26.9 us -> 28.5 us
    pallas_call x7, Pallas kernels: 29.2 us -> 25.8 us  [the longest x2 21.4 us: expert_call(): pl.pallas_call(lambda *refs: expert_kernel(layer, *refs), out_shape=shape...]
    all_to_all x2, waiting for transfers between devices: 24.4 us -> 26 us  [exchange(): lax.all_to_all(packed.reshape(EXPERTS, PACK, WIDE), 'ep', split_axis=0, c...]
  transfers between devices with their start and end apart: 9 -> 9, of which waited for: 5 -> 5; matrix products, arithmetic and copies ran while one was open for 0% -> 0% of each run, Pallas kernels for 6% -> 5%
where the time goes in v4:
time: 124 us
  blocking collectives  43.8 us (35%)
  waiting for transfers between devices  28.5 us (23%)
  Pallas kernels  27.7 us (22%)
  starting transfers between devices  22 us (18%)
    all_to_all x2, blocking collectives, exchange(): lax.all_to_all(packed.reshape(EXPERTS, PACK, WIDE), 'ep', split_axis=0, c...  43.8 us
    all_to_all x2, waiting for transfers between devices, exchange(): lax.all_to_all(packed.reshape(EXPERTS, PACK, WIDE), 'ep', split_axis=0, c...  26 us
    pallas_call x2, Pallas kernels, expert_call(): pl.pallas_call(lambda *refs: expert_kernel(layer, *refs), out_shape=shape...  21.4 us
    ppermute x6, starting transfers between devices, swapped(): return lax.ppermute(value, 'section', [(0, 1), (1, 0)])  10.6 us
    all_to_all x2, starting transfers between devices, exchange(): lax.all_to_all(packed.reshape(EXPERTS, PACK, WIDE), 'ep', split_axis=0, c...  10.1 us
  transfers between devices with their start and end apart: 9, of which 5 were waited for; matrix products, arithmetic and copies ran while one was open for 0% of the time, Pallas kernels for 5%

profile of v4, /device:TPU:1, one launch (start us, length us, event | category | flops | bytes accessed | tf_op | source)
XLA Modules:
  0.0 124.0 jit_solution(5048078023280865218)
XLA Ops:
  0.0 1.4 %collective-permute-start = (s32[2,4,64]{2,1,0:T(4,128)}, s32[2,4,64]{2,1,0:T(4,128)S(1)}, u32[]{:S(2)}, u32[]{:S(2)}) collective-permute-start(s32[2,4,64]{2,1,0:T(4,128)} %bitcast.32), channel_id=1, source_target_pairs={{0,64},{64,0},{1,65},{65,1},{2,66},{66,2},{3,67},{67,3},{4,68},{68... | collective-permute-start | bytes 6152 | tf_op jit(solution)/shard_map/ppermute | solution.py:428
  1.4 0.0 collective-permute-start.1
  1.4 1.0 collective-permute-done.refs_2_.got_ids
  2.5 0.3 collective-permute-done.1.refs_3_.got_w
  2.8 0.2 collective-permute-start.4
  3.0 0.3 collective-permute-start.3
  3.3 0.0 copy-start
  3.3 1.8 %other_pre.1 = bf16[384,3072]{1,0:T(8,128)(2,1)S(1)} custom-call(bf16[2,384,3072]{2,1,0:T(8,128)(2,1)} %bitcast.23), custom_call_target="tpu_custom_call" | custom-call | flops 1000000 | bytes 4000000 | tf_op jit(solution)/shard_map/other_pre/pallas_call | solution.py:446
  5.1 0.0 copy-start.2
  5.1 0.0 copy-start.3
  5.1 0.2 collective-permute-start.2
  5.4 1.0 copy-done
  6.4 0.1 lower_factors.1
  6.5 0.0 copy-done.2
  6.5 0.0 copy-done.3
  6.6 1.6 %send_first.1 = (bf16[512,1152]{1,0:T(8,128)(2,1)S(1)}, bf16[64,1536]{1,0:T(8,128)(2,1)S(1)}) custom-call(s32[2,4,64]{2,1,0:T(4,128)S(1)} %bitcast.34, f32[2,4,64]{2,1,0:T(4,128)S(1)} %bitcast.38, s32[2,4,64]{2,1,0:T(4,128)S(1)} %collective-permute-done.refs_2_.got_ids, f32[2,4,64]{2,1,0:T(4,128)S(1)} %collective-permute-done.1.refs_3_.got_w, ...), custom_call_target="tpu_custom_call" | custom-call | flops 300000000 | bytes 4000000 | tf_op jit(solution)/shard_map/send_first/pallas_call | solution.py:457
  8.1 25.5 %all_to_all.20 = bf16[64,8,1152]{2,1,0:T(8,128)(2,1)S(1)} all-to-all(bf16[64,8,1152]{2,1,0:T(8,128)(2,1)S(1)} %bitcast.31), channel_id=1, replica_groups=mesh['section'=2,'ep'=64] {'ep'}, dimensions={0} | all-to-all | bytes 2359296 | tf_op jit(solution)/shard_map/all_to_all | solution.py:422
  33.7 0.0 collective-permute-done.2.refs_2_
  33.7 0.0 collective-permute-done.3.refs_4_
  33.7 0.0 collective-permute-done.4.refs_6_
  33.7 10.8 %expert_layer_1.1 = bf16[512,1152]{1,0:T(8,128)(2,1)} custom-call(bf16[512,1152]{1,0:T(8,128)(2,1)S(1)} %bitcast.26, bf16[2,384,3072]{2,1,0:T(8,128)(2,1)} %bitcast.24, bf16[384,3072]{1,0:T(8,128)(2,1)S(1)} %collective-permute-done.2.refs_2_, bf16[1536,1536]{1,0:T(8,128)(2,1)} %bitcast.44, bf16[1536,1536]{1,0:T(8,128)(2,1)} %collective-permute-done.3.refs_4_, ...), custom_call_target="tpu_custom_call" | custom-call | flops 5435817984 | bytes 20000000 | tf_op jit(solution)/shard_map/expert_layer_1/pallas_call | solution.py:399
  44.5 5.4 %all-to-all-start.1 = ((bf16[64,8,1152]{2,1,0:T(8,128)(2,1)}), bf16[64,8,1152]{2,1,0:T(8,128)(2,1)S(1)}, u32[]{:S(2)}, u32[]{:S(2)}) async-start(bf16[64,8,1152]{2,1,0:T(8,128)(2,1)} %bitcast.11), calls=%async_computation.1 | async-start | bytes 2359296 | tf_op jit(solution)/shard_map/all_to_all | solution.py:422
  50.0 1.3 %collective-permute-start.5 = (bf16[384,3072]{1,0:T(8,128)(2,1)}, bf16[384,3072]{1,0:T(8,128)(2,1)}, u32[]{:S(2)}, u32[]{:S(2)}) collective-permute-start(bf16[384,3072]{1,0:T(8,128)(2,1)} %get-tuple-element.44), channel_id=1, source_target_pairs={{0,64},{1,65},{2,66},{3,67},{4,68},{5,69},{6,70},{7,71},{8,72},{9,... | collective-permute-start | bytes 7077896 | tf_op jit(solution)/shard_map/ppermute | solution.py:471
  51.3 1.5 %routes_section_1.1 = (bf16[3,512,256]{2,1,0:T(8,128)(2,1)S(1)}, bf16[3,128,512]{2,1,0:T(8,128)(2,1)S(1)}, bf16[3,128,512]{2,1,0:T(8,128)(2,1)S(1)}) custom-call(s32[2,4,64]{2,1,0:T(4,128)S(1)} %bitcast.35, f32[2,4,64]{2,1,0:T(4,128)S(1)} %bitcast.39, ...), custom_call_target="tpu_custom_call", output_to_operand_aliasing={{0}: (4, {}), {1}: (5, {}), {2}: (6, {})} | custom-call | flops 1000000000 | bytes 4000000 | tf_op jit(solution)/shard_map/routes_section_1/pallas_call | solution.py:384
  52.7 11.8 %all-to-all-done.1 = bf16[64,8,1152]{2,1,0:T(8,128)(2,1)S(1)} async-done(((bf16[64,8,1152]{2,1,0:T(8,128)(2,1)}), bf16[64,8,1152]{2,1,0:T(8,128)(2,1)S(1)}, u32[]{:S(2)}, u32[]{:S(2)}) %all-to-all-start.1) | async-done | bytes 1179680 | tf_op jit(solution)/shard_map/all_to_all | solution.py:422
  64.6 0.0 copy-start.1
  64.6 0.9 relay.1
  65.5 18.2 %all_to_all.21 = bf16[64,8,1152]{2,1,0:T(8,128)(2,1)S(1)} all-to-all(bf16[64,8,1152]{2,1,0:T(8,128)(2,1)S(1)} %bitcast.30), channel_id=1, replica_groups=mesh['section'=2,'ep'=64] {'ep'}, dimensions={0} | all-to-all | bytes 2359296 | tf_op jit(solution)/shard_map/all_to_all | solution.py:422
  83.8 0.0 collective-permute-done.5.refs_2_
  83.8 0.0 copy-done.1
  83.8 10.6 %expert_layer_0.1 = bf16[512,1152]{1,0:T(8,128)(2,1)} custom-call(bf16[512,1152]{1,0:T(8,128)(2,1)S(1)} %bitcast.27, bf16[384,3072]{1,0:T(8,128)(2,1)S(1)} %copy-done.1, bf16[384,3072]{1,0:T(8,128)(2,1)} %collective-permute-done.5.refs_2_, bf16[1536,1536]{1,0:T(8,128)(2,1)} %bitcast.45, bf16[1536,1536]{1,0:T(8,128)(2,1)} %collective-permute-done.3.refs_4_, ...), custom_call_target="tpu_custom_call" | custom-call | flops 5435817984 | bytes 20000000 | tf_op jit(solution)/shard_map/expert_layer_0/pallas_call | solution.py:399
  94.4 4.7 %all-to-all-start.3 = ((bf16[64,8,1152]{2,1,0:T(8,128)(2,1)}), bf16[64,8,1152]{2,1,0:T(8,128)(2,1)S(1)}, u32[]{:S(2)}, u32[]{:S(2)}) async-start(bf16[64,8,1152]{2,1,0:T(8,128)(2,1)} %bitcast.15), calls=%async_computation.3 | async-start | bytes 2359296 | tf_op jit(solution)/shard_map/all_to_all | solution.py:422
  99.1 14.2 %all-to-all-done.3 = bf16[64,8,1152]{2,1,0:T(8,128)(2,1)S(1)} async-done(((bf16[64,8,1152]{2,1,0:T(8,128)(2,1)}), bf16[64,8,1152]{2,1,0:T(8,128)(2,1)S(1)}, u32[]{:S(2)}, u32[]{:S(2)}) %all-to-all-start.3) | async-done | bytes 1179680 | tf_op jit(solution)/shard_map/all_to_all | solution.py:422
  113.3 0.4 gather_last.1
  113.7 8.4 %collective-permute-start.6 = (bf16[64,1536]{1,0:T(8,128)(2,1)S(1)}, bf16[64,1536]{1,0:T(8,128)(2,1)S(1)}, u32[]{:S(2)}, u32[]{:S(2)}) collective-permute-start(bf16[64,1536]{1,0:T(8,128)(2,1)S(1)} %broadcast_select_fusion), channel_id=1, source_target_pairs={{0,64},{64,0},{1,65},{65,1},{2,66},{66,2},{3,67},{67,3},{4,68},{68... | collective-permute-start | bytes 589832 | tf_op jit(solution)/shard_map/ppermute | solution.py:428
  122.1 1.1 collective-permute-done.6
  123.2 0.8 maximum_bitcast_fusion
  (3 shorter events, 0.1 us)
Async XLA Ops:
  0.0 2.5 %collective-permute-start = (s32[2,4,64]{2,1,0:T(4,128)}, s32[2,4,64]{2,1,0:T(4,128)S(1)}, u32[]{:S(2)}, u32[]{:S(2)}) collective-permute-start(s32[2,4,64]{2,1,0:T(4,128)} %bitcast.32), channel_id=1, source_target_pairs={{0,64},{64,0},{1,65},{65,1},{2,66},{66,2},{3,67},{67,3},{4,68},{68... | collective-permute-start | bytes 6152 | tf_op jit(solution)/shard_map/ppermute | solution.py:428
  1.4 1.4 %collective-permute-start.1 = (f32[2,4,64]{2,1,0:T(4,128)}, f32[2,4,64]{2,1,0:T(4,128)S(1)}, u32[]{:S(2)}, u32[]{:S(2)}) collective-permute-start(f32[2,4,64]{2,1,0:T(4,128)} %bitcast.36), channel_id=1, source_target_pairs={{0,64},{64,0},{1,65},{65,1},{2,66},{66,2},{3,67},{67,3},{4,68},{68... | collective-permute-start | bytes 6152 | tf_op jit(solution)/shard_map/ppermute | solution.py:428
  2.8 30.9 %collective-permute-start.4 = (bf16[1536,3072]{1,0:T(8,128)(2,1)}, bf16[1536,3072]{1,0:T(8,128)(2,1)}, u32[]{:S(2)}, u32[]{:S(2)}) collective-permute-start(bf16[1536,3072]{1,0:T(8,128)(2,1)} %bitcast.40), channel_id=1, source_target_pairs={{0,64},{64,0},{1,65},{65,1},{2,66},{66,2},{3,67},{67,3},{4,68},{68... | collective-permute-start | bytes 28311560 | tf_op jit(solution)/shard_map/ppermute | solution.py:428
  3.0 30.7 %collective-permute-start.3 = (bf16[1536,1536]{1,0:T(8,128)(2,1)}, bf16[1536,1536]{1,0:T(8,128)(2,1)}, u32[]{:S(2)}, u32[]{:S(2)}) collective-permute-start(bf16[1536,1536]{1,0:T(8,128)(2,1)} %bitcast.43), channel_id=1, source_target_pairs={{0,64},{64,0},{1,65},{65,1},{2,66},{66,2},{3,67},{67,3},{4,68},{68... | collective-permute-start | bytes 14155784 | tf_op jit(solution)/shard_map/ppermute | solution.py:428
  3.3 3.0 %copy-start = (bf16[1,2,1,384,3072]{4,3,2,1,0:T(8,128)(2,1)S(1)}, bf16[1,2,1,384,3072]{4,3,2,1,0:T(8,128)(2,1)}, u32[]{:S(2)}) copy-start(bf16[1,2,1,384,3072]{4,3,2,1,0:T(8,128)(2,1)} %param.9) | copy-start | bytes 14155780
  5.1 1.4 %copy-start.2 = (s32[1,2,64,4]{2,3,1,0:T(4,128)S(1)}, s32[1,2,64,4]{2,3,1,0:T(4,128)}, u32[]{:S(2)}) copy-start(s32[1,2,64,4]{2,3,1,0:T(4,128)} %param.7) | copy-start | bytes 6148
  5.1 1.4 %copy-start.3 = (f32[1,2,64,4]{2,3,1,0:T(4,128)S(1)}, f32[1,2,64,4]{2,3,1,0:T(4,128)}, u32[]{:S(2)}) copy-start(f32[1,2,64,4]{2,3,1,0:T(4,128)} %param.8) | copy-start | bytes 6148
  5.1 28.6 %collective-permute-start.2 = (bf16[384,3072]{1,0:T(8,128)(2,1)S(1)}, bf16[384,3072]{1,0:T(8,128)(2,1)S(1)}, u32[]{:S(2)}, u32[]{:S(2)}) collective-permute-start(bf16[384,3072]{1,0:T(8,128)(2,1)S(1)} %other_pre.1), channel_id=1, source_target_pairs={{0,64},{64,0},{1,65},{65,1},{2,66},{66,2},{3,67},{67,3},{4,68},{68... | collective-permute-start | bytes 7077896 | tf_op jit(solution)/shard_map/ppermute | solution.py:428
  44.5 20.1 %all-to-all-start.1 = ((bf16[64,8,1152]{2,1,0:T(8,128)(2,1)}), bf16[64,8,1152]{2,1,0:T(8,128)(2,1)S(1)}, u32[]{:S(2)}, u32[]{:S(2)}) async-start(bf16[64,8,1152]{2,1,0:T(8,128)(2,1)} %bitcast.11), calls=%async_computation.1 | async-start | bytes 2359296 | tf_op jit(solution)/shard_map/all_to_all | solution.py:422
  50.0 33.8 %collective-permute-start.5 = (bf16[384,3072]{1,0:T(8,128)(2,1)}, bf16[384,3072]{1,0:T(8,128)(2,1)}, u32[]{:S(2)}, u32[]{:S(2)}) collective-permute-start(bf16[384,3072]{1,0:T(8,128)(2,1)} %get-tuple-element.44), channel_id=1, source_target_pairs={{0,64},{1,65},{2,66},{3,67},{4,68},{5,69},{6,70},{7,71},{8,72},{9,... | collective-permute-start | bytes 7077896 | tf_op jit(solution)/shard_map/ppermute | solution.py:471
  64.6 19.2 %copy-start.1 = (bf16[384,3072]{1,0:T(8,128)(2,1)S(1)}, bf16[384,3072]{1,0:T(8,128)(2,1)}, u32[]{:S(2)}) copy-start(bf16[384,3072]{1,0:T(8,128)(2,1)} %get-tuple-element.27.refs_1_) | copy-start | bytes 7077892
  94.4 18.9 %all-to-all-start.3 = ((bf16[64,8,1152]{2,1,0:T(8,128)(2,1)}), bf16[64,8,1152]{2,1,0:T(8,128)(2,1)S(1)}, u32[]{:S(2)}, u32[]{:S(2)}) async-start(bf16[64,8,1152]{2,1,0:T(8,128)(2,1)} %bitcast.15), calls=%async_computation.3 | async-start | bytes 2359296 | tf_op jit(solution)/shard_map/all_to_all | solution.py:422
  113.7 9.5 %collective-permute-start.6 = (bf16[64,1536]{1,0:T(8,128)(2,1)S(1)}, bf16[64,1536]{1,0:T(8,128)(2,1)S(1)}, u32[]{:S(2)}, u32[]{:S(2)}) collective-permute-start(bf16[64,1536]{1,0:T(8,128)(2,1)S(1)} %broadcast_select_fusion), channel_id=1, source_target_pairs={{0,64},{64,0},{1,65},{65,1},{2,66},{66,2},{3,67},{67,3},{4,68},{68... | collective-permute-start | bytes 589832 | tf_op jit(solution)/shard_map/ppermute | solution.py:428

commit v5 on v4

--- a/solution.py
+++ b/solution.py
@@ -31,6 +31,7 @@
 PIECES = 4
 BIG = 48 * 1024 * 1024
 EXPERT_BIG = 48 * 1024 * 1024
+FACTORS_BIG = 58 * 1024 * 1024
 SMALL = 16 * 1024 * 1024
 
 
@@ -206,7 +207,7 @@
 
 
 def routes_kernel(mine, own_ids, own_w, got_ids, got_w, *refs):
-    send, gather_one, gather_zero, ids_one, ids_zero, weights, sem = refs[-7:]
+    send, gather_one, zero_out, ids_one, ids_zero, weights, gather_zero, sem = refs[-8:]
     one = got_ids if mine == 0 else own_ids
     ids, w = (own_ids, own_w) if mine == 0 else (got_ids, got_w)
 
@@ -221,12 +222,16 @@
             copy.start()
         for copy in picks:
             copy.wait()
-        for ids_held, target in ((ids_one, gather_one), (ids_zero, gather_zero)):
-            for part, mask in enumerate(gather_masks(lanes(ids_held[...].astype(F32), 2))):
-                target[part] = mask.T.astype(BF)
+        away = pltpu.make_async_copy(gather_zero, zero_out, sem.at[3])
+        for part, mask in enumerate(gather_masks(lanes(ids_zero[...].astype(F32), 2))):
+            gather_zero[part] = mask.T.astype(BF)
+        away.start()
+        for part, mask in enumerate(gather_masks(lanes(ids_one[...].astype(F32), 2))):
+            gather_one[part] = mask.T.astype(BF)
         masks = send_masks(lanes(ids_zero[...].astype(F32), 4), lanes(weights[...], 4))
         for part, mask in enumerate(masks):
             send[part] = mask
+        away.wait()
 
 
 def relay_kernel(packed_ref, gather, send, grads, lower_ref, out_ref):
@@ -377,22 +382,24 @@
         "lower_factors",
         20_000_000,
         [FAR] * 2,
-    )(pre)
+        limit=FACTORS_BIG,
+    )(in_hbm(pre))
 
 
 def routes_call(mine, picks, masks):
+    held = [in_vmem(mask) for mask in masks[:2]] + [in_hbm(mask) for mask in masks[2:]]
     return small_call(
         lambda *refs: routes_kernel(mine, *refs),
-        [pltpu.VMEM(dims, BF) for dims in MASKS],
-        [FAR] * 4 + [NEAR] * len(masks),
-        [PICK_IDS, PICK_IDS, PICK_WEIGHTS],
-        (3,),
+        [pltpu.VMEM(MASKS[0], BF), pltpu.VMEM(MASKS[1], BF), pltpu.HBM(MASKS[2], BF)],
+        [FAR] * 4 + [NEAR, NEAR, FAR][: len(masks)],
+        [PICK_IDS, PICK_IDS, PICK_WEIGHTS, pltpu.VMEM(MASKS[2], BF)],
+        (4,),
         f"routes_section_{mine}",
         1_000_000_000,
-        [NEAR] * 3,
+        [NEAR, NEAR, FAR],
         limit=SMALL,
         aliases={4 + place: place for place in range(len(masks))},
-    )(*picks, *[in_vmem(mask) for mask in masks])
+    )(*picks, *held)
 
 
 def expert_call(layer, *operands):

time: 124 us -> 125 us (level)
  blocking collectives: 43.8 us -> 45.4 us
    ppermute x6, starting transfers between devices: 10.6 us -> 8.6 us  [swapped(): return lax.ppermute(value, 'section', [(0, 1), (1, 0)])]
    all_to_all x2, blocking collectives: 43.8 us -> 45.4 us  [exchange(): lax.all_to_all(packed.reshape(EXPERTS, PACK, WIDE), 'ep', split_axis=0, c...]
where the time goes in v5:
time: 125 us
  blocking collectives  45.4 us (36%)
  waiting for transfers between devices  28.9 us (23%)
  Pallas kernels  27.9 us (22%)
  starting transfers between devices  21.2 us (17%)
    all_to_all x2, blocking collectives, exchange(): lax.all_to_all(packed.reshape(EXPERTS, PACK, WIDE), 'ep', split_axis=0, c...  45.4 us
    all_to_all x2, waiting for transfers between devices, exchange(): lax.all_to_all(packed.reshape(EXPERTS, PACK, WIDE), 'ep', split_axis=0, c...  26.4 us
    pallas_call x2, Pallas kernels, expert_call(): pl.pallas_call(lambda *refs: expert_kernel(layer, *refs), out_shape=shape...  21.4 us
    all_to_all x2, starting transfers between devices, exchange(): lax.all_to_all(packed.reshape(EXPERTS, PACK, WIDE), 'ep', split_axis=0, c...  11.3 us
    ppermute x6, starting transfers between devices, swapped(): return lax.ppermute(value, 'section', [(0, 1), (1, 0)])  8.6 us
  transfers between devices with their start and end apart: 9, of which 5 were waited for; matrix products, arithmetic and copies ran while one was open for 0% of the time, Pallas kernels for 5%

profile of v5, /device:TPU:1, one launch (start us, length us, event | category | flops | bytes accessed | tf_op | source)
XLA Modules:
  0.0 124.6 jit_solution(15402529083667835331)
XLA Ops:
  0.0 1.4 %collective-permute-start = (s32[2,4,64]{2,1,0:T(4,128)}, s32[2,4,64]{2,1,0:T(4,128)S(1)}, u32[]{:S(2)}, u32[]{:S(2)}) collective-permute-start(s32[2,4,64]{2,1,0:T(4,128)} %bitcast.29), channel_id=1, source_target_pairs={{0,64},{64,0},{1,65},{65,1},{2,66},{66,2},{3,67},{67,3},{4,68},{68... | collective-permute-start | bytes 6152 | tf_op jit(solution)/shard_map/ppermute | solution.py:435
  1.4 0.0 collective-permute-start.1
  1.4 1.0 collective-permute-done.refs_2_.got_ids
  2.5 0.3 collective-permute-done.1.refs_3_.got_w
  2.8 0.2 collective-permute-start.4
  3.0 0.3 collective-permute-start.3
  3.3 1.6 %other_pre.1 = bf16[384,3072]{1,0:T(8,128)(2,1)S(1)} custom-call(bf16[2,384,3072]{2,1,0:T(8,128)(2,1)} %bitcast.37), custom_call_target="tpu_custom_call" | custom-call | flops 1000000 | bytes 4000000 | tf_op jit(solution)/shard_map/other_pre/pallas_call | solution.py:453
  4.9 0.0 copy-start.2
  5.0 0.0 copy-start.3
  5.0 0.2 collective-permute-start.2
  5.2 0.1 lower_factors.1
  5.4 0.3 copy-done.2
  5.6 0.0 copy-done.3
  5.7 1.6 %send_first.1 = (bf16[512,1152]{1,0:T(8,128)(2,1)S(1)}, bf16[64,1536]{1,0:T(8,128)(2,1)S(1)}) custom-call(s32[2,4,64]{2,1,0:T(4,128)S(1)} %bitcast.31, f32[2,4,64]{2,1,0:T(4,128)S(1)} %bitcast.35, s32[2,4,64]{2,1,0:T(4,128)S(1)} %collective-permute-done.refs_2_.got_ids, f32[2,4,64]{2,1,0:T(4,128)S(1)} %collective-permute-done.1.refs_3_.got_w, ...), custom_call_target="tpu_custom_call" | custom-call | flops 300000000 | bytes 4000000 | tf_op jit(solution)/shard_map/send_first/pallas_call | solution.py:464
  7.3 25.4 %all_to_all.20 = bf16[64,8,1152]{2,1,0:T(8,128)(2,1)S(1)} all-to-all(bf16[64,8,1152]{2,1,0:T(8,128)(2,1)S(1)} %bitcast.28), channel_id=1, replica_groups=mesh['section'=2,'ep'=64] {'ep'}, dimensions={0} | all-to-all | bytes 2359296 | tf_op jit(solution)/shard_map/all_to_all | solution.py:429
  32.7 0.0 collective-permute-done.2.refs_2_
  32.7 0.0 collective-permute-done.3.refs_4_
  32.7 0.0 collective-permute-done.4.refs_6_
  32.7 10.8 %expert_layer_1.1 = bf16[512,1152]{1,0:T(8,128)(2,1)} custom-call(bf16[512,1152]{1,0:T(8,128)(2,1)S(1)} %bitcast.23, bf16[2,384,3072]{2,1,0:T(8,128)(2,1)} %bitcast.39, bf16[384,3072]{1,0:T(8,128)(2,1)S(1)} %collective-permute-done.2.refs_2_, bf16[1536,1536]{1,0:T(8,128)(2,1)} %bitcast.44, bf16[1536,1536]{1,0:T(8,128)(2,1)} %collective-permute-done.3.refs_4_, ...), custom_call_target="tpu_custom_call" | custom-call | flops 5435817984 | bytes 20000000 | tf_op jit(solution)/shard_map/expert_layer_1/pallas_call | solution.py:406
  43.5 6.5 %all-to-all-start.1 = ((bf16[64,8,1152]{2,1,0:T(8,128)(2,1)}), bf16[64,8,1152]{2,1,0:T(8,128)(2,1)S(1)}, u32[]{:S(2)}, u32[]{:S(2)}) async-start(bf16[64,8,1152]{2,1,0:T(8,128)(2,1)} %bitcast.11), calls=%async_computation.1 | async-start | bytes 2359296 | tf_op jit(solution)/shard_map/all_to_all | solution.py:429
  50.0 1.3 %collective-permute-start.5 = (bf16[384,3072]{1,0:T(8,128)(2,1)}, bf16[384,3072]{1,0:T(8,128)(2,1)}, u32[]{:S(2)}, u32[]{:S(2)}) collective-permute-start(bf16[384,3072]{1,0:T(8,128)(2,1)} %get-tuple-element.44), channel_id=1, source_target_pairs={{0,64},{1,65},{2,66},{3,67},{4,68},{5,69},{6,70},{7,71},{8,72},{9,... | collective-permute-start | bytes 7077896 | tf_op jit(solution)/shard_map/ppermute | solution.py:478
  51.3 1.8 %routes_section_1.1 = (bf16[3,512,256]{2,1,0:T(8,128)(2,1)S(1)}, bf16[3,128,512]{2,1,0:T(8,128)(2,1)S(1)}, bf16[3,128,512]{2,1,0:T(8,128)(2,1)}) custom-call(s32[2,4,64]{2,1,0:T(4,128)S(1)} %bitcast.32, f32[2,4,64]{2,1,0:T(4,128)S(1)} %bitcast.36, ...), custom_call_target="tpu_custom_call", output_to_operand_aliasing={{0}: (4, {}), {1}: (5, {}), {2}: (6, {})} | custom-call | flops 1000000000 | bytes 4000000 | tf_op jit(solution)/shard_map/routes_section_1/pallas_call | solution.py:391
  53.0 11.8 %all-to-all-done.1 = bf16[64,8,1152]{2,1,0:T(8,128)(2,1)S(1)} async-done(((bf16[64,8,1152]{2,1,0:T(8,128)(2,1)}), bf16[64,8,1152]{2,1,0:T(8,128)(2,1)S(1)}, u32[]{:S(2)}, u32[]{:S(2)}) %all-to-all-start.1) | async-done | bytes 1179680 | tf_op jit(solution)/shard_map/all_to_all | solution.py:429
  64.8 0.0 copy-start
  64.8 0.9 relay.1
  65.7 20.0 %all_to_all.21 = bf16[64,8,1152]{2,1,0:T(8,128)(2,1)S(1)} all-to-all(bf16[64,8,1152]{2,1,0:T(8,128)(2,1)S(1)} %bitcast.27), channel_id=1, replica_groups=mesh['section'=2,'ep'=64] {'ep'}, dimensions={0} | all-to-all | bytes 2359296 | tf_op jit(solution)/shard_map/all_to_all | solution.py:429
  85.7 0.0 collective-permute-done.5.refs_2_
  85.7 0.0 copy-done
  85.7 10.6 %expert_layer_0.1 = bf16[512,1152]{1,0:T(8,128)(2,1)} custom-call(bf16[512,1152]{1,0:T(8,128)(2,1)S(1)} %bitcast.24, bf16[384,3072]{1,0:T(8,128)(2,1)S(1)} %copy-done, bf16[384,3072]{1,0:T(8,128)(2,1)} %collective-permute-done.5.refs_2_, bf16[1536,1536]{1,0:T(8,128)(2,1)} %bitcast.45, bf16[1536,1536]{1,0:T(8,128)(2,1)} %collective-permute-done.3.refs_4_, ...), custom_call_target="tpu_custom_call" | custom-call | flops 5435817984 | bytes 20000000 | tf_op jit(solution)/shard_map/expert_layer_0/pallas_call | solution.py:406
  96.4 0.0 copy-start.1
  96.4 4.8 %all-to-all-start.3 = ((bf16[64,8,1152]{2,1,0:T(8,128)(2,1)}), bf16[64,8,1152]{2,1,0:T(8,128)(2,1)S(1)}, u32[]{:S(2)}, u32[]{:S(2)}) async-start(bf16[64,8,1152]{2,1,0:T(8,128)(2,1)} %bitcast.15), calls=%async_computation.3 | async-start | bytes 2359296 | tf_op jit(solution)/shard_map/all_to_all | solution.py:429
  101.2 14.7 %all-to-all-done.3 = bf16[64,8,1152]{2,1,0:T(8,128)(2,1)S(1)} async-done(((bf16[64,8,1152]{2,1,0:T(8,128)(2,1)}), bf16[64,8,1152]{2,1,0:T(8,128)(2,1)S(1)}, u32[]{:S(2)}, u32[]{:S(2)}) %all-to-all-start.3) | async-done | bytes 1179680 | tf_op jit(solution)/shard_map/all_to_all | solution.py:429
  115.9 0.0 copy-done.1
  115.9 0.4 gather_last.1
  116.3 6.4 %collective-permute-start.6 = (bf16[64,1536]{1,0:T(8,128)(2,1)S(1)}, bf16[64,1536]{1,0:T(8,128)(2,1)S(1)}, u32[]{:S(2)}, u32[]{:S(2)}) collective-permute-start(bf16[64,1536]{1,0:T(8,128)(2,1)S(1)} %broadcast_select_fusion), channel_id=1, source_target_pairs={{0,64},{64,0},{1,65},{65,1},{2,66},{66,2},{3,67},{67,3},{4,68},{68... | collective-permute-start | bytes 589832 | tf_op jit(solution)/shard_map/ppermute | solution.py:435
  122.7 1.1 collective-permute-done.6
  123.8 0.8 maximum_bitcast_fusion
  (3 shorter events, 0.1 us)
Async XLA Ops:
  0.0 2.5 %collective-permute-start = (s32[2,4,64]{2,1,0:T(4,128)}, s32[2,4,64]{2,1,0:T(4,128)S(1)}, u32[]{:S(2)}, u32[]{:S(2)}) collective-permute-start(s32[2,4,64]{2,1,0:T(4,128)} %bitcast.29), channel_id=1, source_target_pairs={{0,64},{64,0},{1,65},{65,1},{2,66},{66,2},{3,67},{67,3},{4,68},{68... | collective-permute-start | bytes 6152 | tf_op jit(solution)/shard_map/ppermute | solution.py:435
  1.4 1.4 %collective-permute-start.1 = (f32[2,4,64]{2,1,0:T(4,128)}, f32[2,4,64]{2,1,0:T(4,128)S(1)}, u32[]{:S(2)}, u32[]{:S(2)}) collective-permute-start(f32[2,4,64]{2,1,0:T(4,128)} %bitcast.33), channel_id=1, source_target_pairs={{0,64},{64,0},{1,65},{65,1},{2,66},{66,2},{3,67},{67,3},{4,68},{68... | collective-permute-start | bytes 6152 | tf_op jit(solution)/shard_map/ppermute | solution.py:435
  2.8 29.9 %collective-permute-start.4 = (bf16[1536,3072]{1,0:T(8,128)(2,1)}, bf16[1536,3072]{1,0:T(8,128)(2,1)}, u32[]{:S(2)}, u32[]{:S(2)}) collective-permute-start(bf16[1536,3072]{1,0:T(8,128)(2,1)} %bitcast.40), channel_id=1, source_target_pairs={{0,64},{64,0},{1,65},{65,1},{2,66},{66,2},{3,67},{67,3},{4,68},{68... | collective-permute-start | bytes 28311560 | tf_op jit(solution)/shard_map/ppermute | solution.py:435
  3.0 29.7 %collective-permute-start.3 = (bf16[1536,1536]{1,0:T(8,128)(2,1)}, bf16[1536,1536]{1,0:T(8,128)(2,1)}, u32[]{:S(2)}, u32[]{:S(2)}) collective-permute-start(bf16[1536,1536]{1,0:T(8,128)(2,1)} %bitcast.43), channel_id=1, source_target_pairs={{0,64},{64,0},{1,65},{65,1},{2,66},{66,2},{3,67},{67,3},{4,68},{68... | collective-permute-start | bytes 14155784 | tf_op jit(solution)/shard_map/ppermute | solution.py:435
  4.9 0.7 copy-start.2
  5.0 0.7 copy-start.3
  5.0 27.7 %collective-permute-start.2 = (bf16[384,3072]{1,0:T(8,128)(2,1)S(1)}, bf16[384,3072]{1,0:T(8,128)(2,1)S(1)}, u32[]{:S(2)}, u32[]{:S(2)}) collective-permute-start(bf16[384,3072]{1,0:T(8,128)(2,1)S(1)} %other_pre.1), channel_id=1, source_target_pairs={{0,64},{64,0},{1,65},{65,1},{2,66},{66,2},{3,67},{67,3},{4,68},{68... | collective-permute-start | bytes 7077896 | tf_op jit(solution)/shard_map/ppermute | solution.py:435
  43.5 21.3 %all-to-all-start.1 = ((bf16[64,8,1152]{2,1,0:T(8,128)(2,1)}), bf16[64,8,1152]{2,1,0:T(8,128)(2,1)S(1)}, u32[]{:S(2)}, u32[]{:S(2)}) async-start(bf16[64,8,1152]{2,1,0:T(8,128)(2,1)} %bitcast.11), calls=%async_computation.1 | async-start | bytes 2359296 | tf_op jit(solution)/shard_map/all_to_all | solution.py:429
  50.0 35.8 %collective-permute-start.5 = (bf16[384,3072]{1,0:T(8,128)(2,1)}, bf16[384,3072]{1,0:T(8,128)(2,1)}, u32[]{:S(2)}, u32[]{:S(2)}) collective-permute-start(bf16[384,3072]{1,0:T(8,128)(2,1)} %get-tuple-element.44), channel_id=1, source_target_pairs={{0,64},{1,65},{2,66},{3,67},{4,68},{5,69},{6,70},{7,71},{8,72},{9,... | collective-permute-start | bytes 7077896 | tf_op jit(solution)/shard_map/ppermute | solution.py:478
  64.8 20.9 %copy-start = (bf16[384,3072]{1,0:T(8,128)(2,1)S(1)}, bf16[384,3072]{1,0:T(8,128)(2,1)}, u32[]{:S(2)}) copy-start(bf16[384,3072]{1,0:T(8,128)(2,1)} %get-tuple-element.27.refs_1_) | copy-start | bytes 7077892
  96.4 19.5 %copy-start.1 = (bf16[3,128,512]{2,1,0:T(8,128)(2,1)S(1)}, bf16[3,128,512]{2,1,0:T(8,128)(2,1)}, u32[]{:S(2)}) copy-start(bf16[3,128,512]{2,1,0:T(8,128)(2,1)} %get-tuple-element.45.gather) | copy-start | bytes 1179652
  96.4 19.5 %all-to-all-start.3 = ((bf16[64,8,1152]{2,1,0:T(8,128)(2,1)}), bf16[64,8,1152]{2,1,0:T(8,128)(2,1)S(1)}, u32[]{:S(2)}, u32[]{:S(2)}) async-start(bf16[64,8,1152]{2,1,0:T(8,128)(2,1)} %bitcast.15), calls=%async_computation.3 | async-start | bytes 2359296 | tf_op jit(solution)/shard_map/all_to_all | solution.py:429
  116.3 7.5 %collective-permute-start.6 = (bf16[64,1536]{1,0:T(8,128)(2,1)S(1)}, bf16[64,1536]{1,0:T(8,128)(2,1)S(1)}, u32[]{:S(2)}, u32[]{:S(2)}) collective-permute-start(bf16[64,1536]{1,0:T(8,128)(2,1)S(1)} %broadcast_select_fusion), channel_id=1, source_target_pairs={{0,64},{64,0},{1,65},{65,1},{2,66},{66,2},{3,67},{67,3},{4,68},{68... | collective-permute-start | bytes 589832 | tf_op jit(solution)/shard_map/ppermute | solution.py:435
